TPU v7x, 256 devices: a whole 4x4x8 slice. The times are simulated.
256 devices in a mesh: gx: 32 (over x, z), gy: 8 (over y, core).
Axes of the slice: x: 4, y: 4, z: 8, core: 2. Of those that a mesh axis runs over, the one named last changes fastest.
Arguments:
- history: bfloat16 [1, 20, 128, 64, 512], P(None, None, 'gx', 'gy'), may hold values from -6 to 6
- w_point: float32 [20, 20], replicated, may hold values from -1.25 to 1.25
- offset: float32 [20], replicated, may hold values from -3 to 3
- spectral_weight: float32 [2, 20, 20, 128, 24, 24], P(None, None, None, 'gx', 'gy'), may hold values from -3 to 3
- cotangent: bfloat16 [1, 20, 128, 64, 512], P(None, None, 'gx', 'gy'), may hold values from -6 to 6
Outputs:
- activated: bfloat16 [1, 20, 128, 64, 512], P(None, None, 'gx', 'gy')
- grad_history: bfloat16 [1, 20, 128, 64, 512], P(None, None, 'gx', 'gy')
- grad_spectral: float32 [2, 20, 20, 128, 24, 24], P(None, None, None, 'gx', 'gy')
- grad_point: float32 [20, 20], replicated
- grad_offset: float32 [20], replicated
All inputs are finite; a program needn't handle non-finite values.
Results may differ from a plain program's by a relative error of at most 0.0011.
Values sent between devices are 32-bit elements; how exact they have to be, the bound alone decides.
A program may use at most 128 MiB of HBM per device.

v0:
```python
import math

import jax
import jax.numpy as jnp
from jax import lax
from jax.sharding import PartitionSpec as P

MX = 24
MY = 24
MZ = 16
MT = 8
NZ = 64
NT = 8


gelu_coef = 0.7978845608028654
gelu_cubic = 0.044715


def gelu_parts(inputs):
    inner = gelu_coef * (inputs + gelu_cubic * inputs * inputs * inputs)
    smooth = jnp.tanh(inner)
    result = 0.5 * inputs * (1.0 + smooth)
    slope = 0.5 * (1.0 + smooth) + 0.5 * inputs * (1.0 - smooth * smooth) * gelu_coef * (
        1.0 + 3.0 * gelu_cubic * inputs * inputs
    )
    return (result, slope)


def kept_freqs(length, keep):
    half = keep // 2
    return jnp.concatenate([jnp.arange(half), length - half + jnp.arange(half)])


def phase_tables(positions, length, keep):
    freqs = kept_freqs(length, keep)
    wrapped = positions[:, None] * freqs[None, :] % length
    angles = wrapped.astype(jnp.float32) * (2.0 * math.pi / length)
    return (jnp.cos(angles), jnp.sin(angles))


def depth_tables():
    z_freqs = kept_freqs(NZ, MZ)
    t_freqs = kept_freqs(NT, MT)
    z_part = (jnp.arange(NZ)[:, None] * z_freqs[None, :] % NZ).astype(jnp.float32) / NZ
    t_part = (jnp.arange(NT)[:, None] * t_freqs[None, :] % NT).astype(jnp.float32) / NT
    fraction = z_part[:, None, :, None] + t_part[None, :, None, :]
    angles = (2.0 * math.pi * fraction).reshape(NZ * NT, MZ * MT)
    return (jnp.cos(angles), jnp.sin(angles))


def contract(form, left, right):
    return jnp.einsum(form, left, right, precision=lax.Precision.HIGHEST)


def per_device(history, w_point, offset, spectral_weight, cotangent):
    highest = lax.Precision.HIGHEST
    x_cells = history.shape[2]
    y_cells = history.shape[3]
    x_total = x_cells * lax.axis_size("gx")
    y_total = y_cells * lax.axis_size("gy")
    depth_cos, depth_sin = depth_tables()
    x_cos, x_sin = phase_tables(jnp.arange(x_total), x_total, MX)
    own_rows = lax.axis_index("gy") * y_cells + jnp.arange(y_cells)
    own_cos, own_sin = phase_tables(own_rows, y_total, MY)
    cells_all = float(x_total * y_total * NZ * NT)

    def analyse(inputs):
        depth_real = jnp.dot(inputs, depth_cos, precision=highest)
        depth_imag = -jnp.dot(inputs, depth_sin, precision=highest)
        cols_real, cols_imag = (
            lax.all_to_all(depth_real, "gx", split_axis=4, concat_axis=2, tiled=True),
            lax.all_to_all(depth_imag, "gx", split_axis=4, concat_axis=2, tiled=True),
        )
        kx_real = contract("bcxyq,xk->bckyq", cols_real, x_cos) + contract(
            "bcxyq,xk->bckyq", cols_imag, x_sin
        )
        kx_imag = contract("bcxyq,xk->bckyq", cols_imag, x_cos) - contract(
            "bcxyq,xk->bckyq", cols_real, x_sin
        )
        part_real = contract("bckyq,yj->bckjq", kx_real, own_cos) + contract(
            "bckyq,yj->bckjq", kx_imag, own_sin
        )
        part_imag = contract("bckyq,yj->bckjq", kx_imag, own_cos) - contract(
            "bckyq,yj->bckjq", kx_real, own_sin
        )
        out_real, out_imag = (
            lax.psum_scatter(part_real, "gy", scatter_dimension=2, tiled=True),
            lax.psum_scatter(part_imag, "gy", scatter_dimension=2, tiled=True),
        )
        return (out_real, out_imag)

    def synthesise(spec_real, spec_imag):
        full_real, full_imag = (
            lax.all_gather(spec_real, "gy", axis=2, tiled=True),
            lax.all_gather(spec_imag, "gy", axis=2, tiled=True),
        )
        kx_real = (
            contract("bckjq,yj->bckyq", full_real, own_cos)
            - contract("bckjq,yj->bckyq", full_imag, own_sin)
        ) / y_total
        kx_imag = (
            contract("bckjq,yj->bckyq", full_imag, own_cos)
            + contract("bckjq,yj->bckyq", full_real, own_sin)
        ) / y_total
        cols_real = (
            contract("bckyq,xk->bcxyq", kx_real, x_cos)
            - contract("bckyq,xk->bcxyq", kx_imag, x_sin)
        ) / x_total
        cols_imag = (
            contract("bckyq,xk->bcxyq", kx_imag, x_cos)
            + contract("bckyq,xk->bcxyq", kx_real, x_sin)
        ) / x_total
        depth_real, depth_imag = (
            lax.all_to_all(cols_real, "gx", split_axis=2, concat_axis=4, tiled=True),
            lax.all_to_all(cols_imag, "gx", split_axis=2, concat_axis=4, tiled=True),
        )
        grid = jnp.dot(depth_real, depth_cos.T, precision=highest) - jnp.dot(
            depth_imag, depth_sin.T, precision=highest
        )
        return grid / float(NZ * NT)

    values = history.astype(jnp.float32)
    modes_real, modes_imag = analyse(values)
    weight_real = spectral_weight[0]
    weight_imag = spectral_weight[1]
    mixed_real = contract("oiqkj,bikjq->bokjq", weight_real, modes_real) - contract(
        "oiqkj,bikjq->bokjq", weight_imag, modes_imag
    )
    mixed_imag = contract("oiqkj,bikjq->bokjq", weight_real, modes_imag) + contract(
        "oiqkj,bikjq->bokjq", weight_imag, modes_real
    )
    spectral = synthesise(mixed_real, mixed_imag)
    pre_gelu = (
        contract("oi,bixyq->boxyq", w_point, values) + offset[None, :, None, None, None] + spectral
    )
    activated, gelu_slope = gelu_parts(pre_gelu)
    grad_pre = cotangent.astype(jnp.float32) * gelu_slope
    grad_real, grad_imag = analyse(grad_pre)
    back_real = contract("oiqkj,bokjq->bikjq", weight_real, grad_real) + contract(
        "oiqkj,bokjq->bikjq", weight_imag, grad_imag
    )
    back_imag = contract("oiqkj,bokjq->bikjq", weight_real, grad_imag) - contract(
        "oiqkj,bokjq->bikjq", weight_imag, grad_real
    )
    grad_history = (
        contract("oi,boxyq->bixyq", w_point, grad_pre) + synthesise(back_real, back_imag)
    ).astype(jnp.bfloat16)
    pair_real = (
        contract("bokjq,bikjq->oiqkj", grad_real, modes_real)
        + contract("bokjq,bikjq->oiqkj", grad_imag, modes_imag)
    ) / cells_all
    pair_imag = (
        contract("bokjq,bikjq->oiqkj", grad_imag, modes_real)
        - contract("bokjq,bikjq->oiqkj", grad_real, modes_imag)
    ) / cells_all
    grad_spectral = jnp.stack([pair_real, pair_imag])
    local_point = contract("boxyq,bixyq->oi", grad_pre, values)
    local_offset = jnp.sum(grad_pre, axis=(0, 2, 3, 4))
    grad_point, grad_offset = lax.psum((local_point, local_offset), ("gx", "gy"))
    return (activated.astype(jnp.bfloat16), grad_history, grad_spectral, grad_point, grad_offset)


def solution(mesh):
    return jax.shard_map(
        per_device,
        mesh=mesh,
        in_specs=(
            P(None, None, "gx", "gy", None),
            P(),
            P(),
            P(None, None, None, "gx", "gy", None),
            P(None, None, "gx", "gy", None),
        ),
        out_specs=(
            P(None, None, "gx", "gy", None),
            P(None, None, "gx", "gy", None),
            P(None, None, None, "gx", "gy", None),
            P(),
            P(),
        ),
        check_vma=False,
    )
```

profile of v0, /device:TPU:1, one launch (start us, length us, event | category | flops | bytes accessed | tf_op | source)
XLA Modules:
  0.0 563.3 jit_solution(13376060576720004927)
XLA Ops:
  7.4 17.2 %fusion.1 = (f32[64,8,16,8]{3,2,1,0:T(8,128)}, f32[64,8,16,8]{3,2,1,0:T(8,128)}) fusion(f32[8,8]{1,0:T(8,128)S(1)} %fusion.164, f32[64,16]{1,0:T(8,128)S(1)} %fusion.110), kind=kLoop, calls=%fused_computation.3 | loop fusion | flops 131072 | bytes 528640 | tf_op jit(solution)/shard_map/cos | solution.py:49
  24.6 3.7 reshape.375
  35.0 12.1 %all-to-all-start.1 = ((f32[32,1,2560]{2,1,0:T(1,128)}), f32[32,1,2560]{2,1,0:T(1,128)S(1)}, u32[]{:S(2)}, u32[]{:S(2)}) async-start(f32[32,1,2560]{2,1,0:T(1,128)} %reshape.403), calls=%async_computation.1 | async-start | bytes 655360 | tf_op jit(solution)/shard_map/all_to_all | solution.py:73
  58.4 9.4 %all-to-all-start = ((f32[32,1,2560]{2,1,0:T(1,128)}), f32[32,1,2560]{2,1,0:T(1,128)}, u32[]{:S(2)}, u32[]{:S(2)}) async-start(f32[32,1,2560]{2,1,0:T(1,128)} %reshape.405), calls=%async_computation | async-start | bytes 655360 | tf_op jit(solution)/shard_map/all_to_all | solution.py:72
  104.6 67.7 %all-reduce.12.cloned.1.call-done = (f32[1,20,24,24,4]{3,4,1,0,2:T(4,128)}, f32[1,20,24,24,4]{3,4,1,0,2:T(4,128)}) async-done(((f32[1,20,24,24,4]{3,4,1,0,2:T(4,128)}, f32[1,20,24,24,4]{3,4,1,0,2:T(4,128)}), (f32[1,20,24,24,4]{3,4,1,0,2:T(4,128)}, f32[1,20,24,24,4]{3,4,1,0,2:T(4,128)})) %all-reduce.12.cloned.1.call-update) | async-done | bytes 368656
  174.8 5.3 fusion.9
  180.2 16.0 %all_gather.12 = f32[1,20,24,24,4]{3,4,1,0,2:T(4,128)S(1)} all-gather(f32[1,20,3,24,4]{3,4,1,0,2:T(4,128)S(1)} %fusion.107), channel_id=1, replica_groups=mesh['gx'=32,'gy'=8] {'gy'}, dimensions={2}, use_global_device_ids=true | all-gather | bytes 207360 | tf_op jit(solution)/shard_map/all_gather | solution.py:95
  196.2 5.0 fusion.65
  201.3 14.0 %all_gather.13 = f32[1,20,24,24,4]{3,4,1,0,2:T(4,128)S(1)} all-gather(f32[1,20,3,24,4]{3,4,1,0,2:T(4,128)S(1)} %fusion.106), channel_id=1, replica_groups=mesh['gx'=32,'gy'=8] {'gy'}, dimensions={2}, use_global_device_ids=true | all-gather | bytes 207360 | tf_op jit(solution)/shard_map/all_gather | solution.py:96
  215.3 5.0 fusion.61
  220.3 5.0 fusion.45
  225.3 5.0 fusion.47
  233.4 3.7 reshape.409
  237.0 9.6 %all-to-all-start.3 = ((f32[32,1,2560]{2,1,0:T(1,128)}), f32[32,1,2560]{2,1,0:T(1,128)}, u32[]{:S(2)}, u32[]{:S(2)}) async-start(f32[32,1,2560]{2,1,0:T(1,128)} %reshape.409), calls=%async_computation.3 | async-start | bytes 655360 | tf_op jit(solution)/shard_map/all_to_all | solution.py:116
  249.7 3.7 reshape.407
  253.3 4.1 all-to-all-done.3
  257.4 7.7 %all-to-all-start.2 = ((f32[32,1,2560]{2,1,0:T(1,128)}), f32[32,1,2560]{2,1,0:T(1,128)S(1)}, u32[]{:S(2)}, u32[]{:S(2)}) async-start(f32[32,1,2560]{2,1,0:T(1,128)} %reshape.407), calls=%async_computation.2 | async-start | bytes 655360 | tf_op jit(solution)/shard_map/all_to_all | solution.py:115
  281.6 5.7 %fusion.337 = (f32[20]{0:T(128)}, f32[1,20,4,8,512]{4,3,2,1,0:T(8,128)S(1)}, bf16[1,20,4,8,512]{4,3,2,1,0:T(8,128)(2,1)}) fusion(bf16[1,20,4,8,512]{4,3,2,1,0:T(8,128)(2,1)} %param.9, f32[20,4,8,512]{3,2,1,0:T(8,128)S(1)} %fusion.101, f32[20,4,8,128]{3,2,1,0:T(8,128)S(1)} %copy-done.22, f32[512,128,1,1]{1,0,2,3:T(8,128)S(1)} %copy-done.17, ...), kind=kOutput, calls=%fused_computation.376 | convolution fusion | flops 511836160 | bytes 5832864 | tf_op jit(solution)/shard_map/dot_general | solution.py:118
  295.5 9.2 %all-to-all-start.5 = ((f32[32,1,2560]{2,1,0:T(1,128)}), f32[32,1,2560]{2,1,0:T(1,128)}, u32[]{:S(2)}, u32[]{:S(2)}) async-start(f32[32,1,2560]{2,1,0:T(1,128)} %reshape.411), calls=%async_computation.5 | async-start | bytes 655360 | tf_op jit(solution)/shard_map/all_to_all | solution.py:73
  314.5 8.1 %all-to-all-start.4 = ((f32[32,1,2560]{2,1,0:T(1,128)}), f32[32,1,2560]{2,1,0:T(1,128)}, u32[]{:S(2)}, u32[]{:S(2)}) async-start(f32[32,1,2560]{2,1,0:T(1,128)} %reshape.413), calls=%async_computation.4 | async-start | bytes 655360 | tf_op jit(solution)/shard_map/all_to_all | solution.py:72
  331.9 3.9 fusion.129
  366.8 77.5 %all-reduce.4 = (f32[20,20]{1,0:T(8,128)}, f32[20]{0:T(128)}) all-reduce(f32[20,20]{1,0:T(8,128)S(1)} %fusion.52, f32[20]{0:T(128)S(1)} %copy-done.23), channel_id=1, replica_groups=mesh['gx'=32,'gy'=8] {'gx','gy'}, use_global_device_ids=true, to_apply=%region_4.5 | all-reduce | flops 420 | bytes 3360 | tf_op jit(solution)/shard_map/psum | solution.py:160
  447.4 4.7 fusion.5
  452.2 14.5 %all_gather.14 = f32[1,20,24,24,4]{3,4,1,0,2:T(4,128)S(1)} all-gather(f32[1,20,3,24,4]{3,4,1,0,2:T(4,128)S(1)} %fusion.105), channel_id=1, replica_groups=mesh['gx'=32,'gy'=8] {'gy'}, dimensions={2}, use_global_device_ids=true | all-gather | bytes 207360 | tf_op jit(solution)/shard_map/all_gather | solution.py:95
  466.7 5.0 fusion.59
  471.7 14.0 %all_gather.15 = f32[1,20,24,24,4]{3,4,1,0,2:T(4,128)S(1)} all-gather(f32[1,20,3,24,4]{3,4,1,0,2:T(4,128)S(1)} %fusion.104), channel_id=1, replica_groups=mesh['gx'=32,'gy'=8] {'gy'}, dimensions={2}, use_global_device_ids=true | all-gather | bytes 207360 | tf_op jit(solution)/shard_map/all_gather | solution.py:96
  485.8 5.0 fusion.55
  490.8 5.0 fusion.49
  495.8 5.0 fusion.51
  505.4 3.7 reshape.417
  509.1 6.8 %all-to-all-start.7 = ((f32[32,1,2560]{2,1,0:T(1,128)}), f32[32,1,2560]{2,1,0:T(1,128)S(1)}, u32[]{:S(2)}, u32[]{:S(2)}) async-start(f32[32,1,2560]{2,1,0:T(1,128)} %reshape.417), calls=%async_computation.7 | async-start | bytes 655360 | tf_op jit(solution)/shard_map/all_to_all | solution.py:116
  526.7 8.9 %all-to-all-start.6 = ((f32[32,1,2560]{2,1,0:T(1,128)}), f32[32,1,2560]{2,1,0:T(1,128)S(1)}, u32[]{:S(2)}, u32[]{:S(2)}) async-start(f32[32,1,2560]{2,1,0:T(1,128)} %reshape.415), calls=%async_computation.6 | async-start | bytes 655360 | tf_op jit(solution)/shard_map/all_to_all | solution.py:115
  (184 shorter events, 176.1 us)
Async XLA Ops:
  7.2 257.9 %copy-start = (f32[20,20]{1,0:T(8,128)S(1)}, f32[20,20]{1,0:T(8,128)}, u32[]{:S(2)}) copy-start(f32[20,20]{1,0:T(8,128)} %param.6) | copy-start | bytes 4804
  24.6 4.4 copy-start.8
  35.0 23.4 %all-to-all-start.1 = ((f32[32,1,2560]{2,1,0:T(1,128)}), f32[32,1,2560]{2,1,0:T(1,128)S(1)}, u32[]{:S(2)}, u32[]{:S(2)}) async-start(f32[32,1,2560]{2,1,0:T(1,128)} %reshape.403), calls=%async_computation.1 | async-start | bytes 655360 | tf_op jit(solution)/shard_map/all_to_all | solution.py:73
  50.7 229.6 %copy-start.2 = (f32[512,128,1,1]{1,0,2,3:T(8,128)}, f32[512,128,1,1]{1,0,2,3:T(8,128)S(1)}, u32[]{:S(2)}) copy-start(f32[512,128,1,1]{1,0,2,3:T(8,128)S(1)} %reshape.373) | copy-start | bytes 786436
  58.4 19.5 %all-to-all-start = ((f32[32,1,2560]{2,1,0:T(1,128)}), f32[32,1,2560]{2,1,0:T(1,128)}, u32[]{:S(2)}, u32[]{:S(2)}) async-start(f32[32,1,2560]{2,1,0:T(1,128)} %reshape.405), calls=%async_computation | async-start | bytes 655360 | tf_op jit(solution)/shard_map/all_to_all | solution.py:72
  67.8 104.5 %all-reduce.12.cloned.1.call-start = ((), (), s32[]{:S(2)}) async-start(), calls=%async_computation.9 | async-start | bytes 3932160
  91.2 4.2 copy-start.12
  93.7 1.7 copy-start.13
  102.0 1.4 copy-start.25
  237.0 20.4 %all-to-all-start.3 = ((f32[32,1,2560]{2,1,0:T(1,128)}), f32[32,1,2560]{2,1,0:T(1,128)}, u32[]{:S(2)}, u32[]{:S(2)}) async-start(f32[32,1,2560]{2,1,0:T(1,128)} %reshape.409), calls=%async_computation.3 | async-start | bytes 655360 | tf_op jit(solution)/shard_map/all_to_all | solution.py:116
  249.7 15.4 %copy-start.9 = (bf16[1,20,4,8,512]{4,3,2,1,0:T(8,128)(2,1)S(1)}, bf16[1,20,4,8,512]{4,3,2,1,0:T(8,128)(2,1)}, u32[]{:S(2)}) copy-start(bf16[1,20,4,8,512]{4,3,2,1,0:T(8,128)(2,1)} %param.5) | copy-start | bytes 1966084
  257.4 17.3 %all-to-all-start.2 = ((f32[32,1,2560]{2,1,0:T(1,128)}), f32[32,1,2560]{2,1,0:T(1,128)S(1)}, u32[]{:S(2)}, u32[]{:S(2)}) async-start(f32[32,1,2560]{2,1,0:T(1,128)} %reshape.407), calls=%async_computation.2 | async-start | bytes 655360 | tf_op jit(solution)/shard_map/all_to_all | solution.py:115
  279.5 2.0 copy-start.17
  279.5 2.0 copy-start.22
  279.6 2.0 copy-start.24
  295.5 19.1 %all-to-all-start.5 = ((f32[32,1,2560]{2,1,0:T(1,128)}), f32[32,1,2560]{2,1,0:T(1,128)}, u32[]{:S(2)}, u32[]{:S(2)}) async-start(f32[32,1,2560]{2,1,0:T(1,128)} %reshape.411), calls=%async_computation.5 | async-start | bytes 655360 | tf_op jit(solution)/shard_map/all_to_all | solution.py:73
  314.5 21.2 %all-to-all-start.4 = ((f32[32,1,2560]{2,1,0:T(1,128)}), f32[32,1,2560]{2,1,0:T(1,128)}, u32[]{:S(2)}, u32[]{:S(2)}) async-start(f32[32,1,2560]{2,1,0:T(1,128)} %reshape.413), calls=%async_computation.4 | async-start | bytes 655360 | tf_op jit(solution)/shard_map/all_to_all | solution.py:72
  322.6 121.7 %all-reduce.10.cloned.1.call-start = ((), (), s32[]{:S(2)}) async-start(), calls=%async_computation.8 | async-start | bytes 3932160
  344.8 6.8 %copy-start.11 = (f32[20,128,8,4]{1,0,3,2:T(8,128)S(1)}, f32[20,128,8,4]{1,0,3,2:T(8,128)}, u32[]{:S(2)}) copy-start(f32[20,128,8,4]{1,0,3,2:T(8,128)} %copy.312) | copy-start | bytes 983044
  351.6 4.8 copy-start.14
  363.0 1.4 copy-start.10
  364.3 2.5 copy-start.23
  495.8 5.7 %copy-start.4 = (f32[20,24,8,4]{1,2,3,0:T(8,128)}, f32[20,24,8,4]{1,2,3,0:T(8,128)S(1)}, u32[]{:S(2)}) copy-start(f32[20,24,8,4]{1,2,3,0:T(8,128)S(1)} %fusion.49) | copy-start | bytes 184324
  509.1 10.3 %copy-start.5 = (f32[20,24,8,4]{1,2,3,0:T(8,128)S(1)}, f32[20,24,8,4]{1,2,3,0:T(8,128)}, u32[]{:S(2)}) copy-start(f32[20,24,8,4]{1,2,3,0:T(8,128)} %copy-done.4) | copy-start | bytes 184324
  509.1 17.5 %all-to-all-start.7 = ((f32[32,1,2560]{2,1,0:T(1,128)}), f32[32,1,2560]{2,1,0:T(1,128)S(1)}, u32[]{:S(2)}, u32[]{:S(2)}) async-start(f32[32,1,2560]{2,1,0:T(1,128)} %reshape.417), calls=%async_computation.7 | async-start | bytes 655360 | tf_op jit(solution)/shard_map/all_to_all | solution.py:116
  515.9 4.2 copy-start.7
  522.4 13.2 %copy-start.19 = (f32[4,3,24,20]{2,0,3,1:T(4,128)S(1)}, f32[4,3,24,20]{2,0,3,1:T(4,128)}, u32[]{:S(2)}) copy-start(f32[4,3,24,20]{2,0,3,1:T(4,128)} %get-tuple-element.46) | copy-start | bytes 69124
  522.4 13.2 %copy-start.20 = (f32[4,3,24,20]{2,0,3,1:T(4,128)S(1)}, f32[4,3,24,20]{2,0,3,1:T(4,128)}, u32[]{:S(2)}) copy-start(f32[4,3,24,20]{2,0,3,1:T(4,128)} %get-tuple-element.52) | copy-start | bytes 69124
  522.4 13.2 %copy-start.21 = (f32[4,3,24,20]{2,0,3,1:T(4,128)S(1)}, f32[4,3,24,20]{2,0,3,1:T(4,128)}, u32[]{:S(2)}) copy-start(f32[4,3,24,20]{2,0,3,1:T(4,128)} %get-tuple-element.48) | copy-start | bytes 69124
  526.7 19.4 %all-to-all-start.6 = ((f32[32,1,2560]{2,1,0:T(1,128)}), f32[32,1,2560]{2,1,0:T(1,128)S(1)}, u32[]{:S(2)}, u32[]{:S(2)}) async-start(f32[32,1,2560]{2,1,0:T(1,128)} %reshape.415), calls=%async_computation.6 | async-start | bytes 655360 | tf_op jit(solution)/shard_map/all_to_all | solution.py:115
  550.9 2.1 copy-start.18
  551.8 1.4 copy-start.1
  (4 other events, 3.1 us)
Sparse Core Ops, SparseCore 0:
  103.5 68.8 all-reduce.11
  364.5 70.3 all-reduce.9
where the time goes:
time: 573 us; the launch traced here: 563 us
  blocking collectives  136 us (24%)
  matrix products  107 us (19%)
  local copies, waits for them, and re-layouts  104 us (18%)
  waiting for transfers between devices  77.2 us (13%)
  starting transfers between devices  72.3 us (13%)
  other arithmetic  50.6 us (9%)
  between operations  16.1 us (3%)
    dot_general x35, matrix products, contract(): return jnp.einsum(form, left, right, precision=lax.Precision.HIGHEST)  88.9 us
    psum x1, blocking collectives, per_device(): lax.psum((local_point, local_offset), ('gx', 'gy'))  77.5 us
    unnamed x4, waiting for transfers between devices  67.8 us
    unnamed x69, local copies, waits for them, and re-layouts  52.5 us
    all_gather x2, blocking collectives, synthesise(): lax.all_gather(spec_real, 'gy', axis=2, tiled=True)  30.5 us
    all_gather x2, blocking collectives, synthesise(): lax.all_gather(spec_imag, 'gy', axis=2, tiled=True)  28.1 us
    all_to_all x2, starting transfers between devices, analyse(): lax.all_to_all(depth_imag, 'gx', split_axis=4, concat_axis=2, tiled=True)  21.2 us
    another operation x16, local copies, waits for them, and re-layouts  17.9 us
  transfers between devices with their start and end apart: 10, of which 6 were waited for; matrix products, arithmetic and copies ran while one was open for 14% of the time, Pallas kernels for 0%

commit v1 on v0

v1 whole, which is shorter than its diff:
```python
import functools

import jax
import jax.numpy as jnp
import ml_dtypes
import numpy as np
from jax import lax
from jax.experimental import pallas as pl
from jax.experimental.pallas import tpu as pltpu
from jax.sharding import PartitionSpec as P

MESH = pl.DeviceIdType.MESH
F32 = jnp.float32
BF16 = jnp.bfloat16
C = 20
NX, NY, NZ, NT = 128, 64, 64, 8
MX, MY, MZ, MT = 24, 24, 16, 8
GX, GY = 32, 8
XC, YC = NX // GX, NY // GY
KX = MX // GY
Q = MZ * MT // GX
ROWS = C * YC
CELLS = NX * NY * NZ * NT
XPOS, ZPOS = 4, 8
gelu_coef = 0.7978845608028654
gelu_cubic = 0.044715


def kept(length, keep):
    half = keep // 2
    return np.concatenate([np.arange(half), length - half + np.arange(half)])


def halves(table):
    table = np.asarray(table, np.float64)
    hi = table.astype(np.float32).astype(ml_dtypes.bfloat16)
    lo = (table - hi.astype(np.float64)).astype(np.float32).astype(ml_dtypes.bfloat16)
    return np.stack([hi, lo])


def depth_table():
    fz, ft = kept(NZ, MZ), kept(NT, MT)
    z, t = np.arange(NZ), np.arange(NT)
    turn = (fz[:, None, None, None] * z[None, None, :, None] % NZ) / NZ + (
        ft[None, :, None, None] * t[None, None, None, :] % NT
    ) / NT
    angle = 2 * np.pi * turn.reshape(GX, 1, Q, NZ * NT)
    return np.concatenate([np.cos(angle), -np.sin(angle)], axis=1).reshape(GX * 2 * Q, NZ * NT)


def x_table():
    fx = kept(NX, MX).reshape(GY, KX)
    x = np.arange(NX).reshape(GX, XC)
    angle = 2 * np.pi * (x[:, :, None, None] * fx[None, None] % NX) / NX
    cos, sin = np.cos(angle), np.sin(angle)
    out = np.zeros((XC, GX, 2, Q, GY, 2, 4, Q))
    for q in range(Q):
        part = out[:, :, :, q, :, :, :KX, q]
        part[:, :, 0, :, 0] = cos.transpose(1, 0, 2, 3)
        part[:, :, 1, :, 0] = sin.transpose(1, 0, 2, 3)
        part[:, :, 0, :, 1] = -sin.transpose(1, 0, 2, 3)
        part[:, :, 1, :, 1] = cos.transpose(1, 0, 2, 3)
    return out.reshape(XC, GX * 2 * Q, GY * 2 * 4 * Q)


def y_table():
    fy = kept(NY, MY)
    angle = 2 * np.pi * (np.arange(NY)[:, None] * fy[None] % NY) / NY
    cos, sin = np.cos(angle), np.sin(angle)
    out = np.zeros((2, NY, 2, 128))
    out[0, :, 0, :MY] = cos
    out[1, :, 0, :MY] = sin
    out[0, :, 1, :MY] = -sin
    out[1, :, 1, :MY] = cos
    return out.reshape(2 * NY, 256)


def split(value):
    hi = value.astype(BF16)
    return hi, (value - hi.astype(F32)).astype(BF16)


def dot(a, b, dims):
    return lax.dot_general(a, b, (dims, ((), ())), preferred_element_type=F32)


NN = ((1,), (0,))
NTD = ((1,), (1,))


def dot3(a, b, dims=NN):
    return dot(a[0], b[0], dims) + (dot(a[0], b[1], dims) + dot(a[1], b[0], dims))


def exact(a, b, dims=NN):
    return lax.dot_general(
        a, b, (dims, ((), ())), precision=lax.Precision.HIGHEST, preferred_element_type=F32
    )


def swap_groups(parts):
    parts = list(parts)
    group = lax.broadcasted_iota(jnp.int32, parts[0].shape, 1) // 8
    for s in (8, 4, 2, 1):
        low = lax.rem(group // s, 2) == 0
        for i in range(16):
            if i & s:
                continue
            a, b = parts[i], parts[i + s]
            parts[i] = jnp.where(low, a, pltpu.roll(b, 8 * s, 1))
            parts[i + s] = jnp.where(low, pltpu.roll(a, 128 - 8 * s, 1), b)
    return parts


def kernel(
    hist, cot, wpt, off, w_hbm, dtab, xa, xs, ya, ys,
    act, ghist, gs_hbm, gpoint, goff,
    w_v, wp, gs_v, vb, base, gpre, sendx, recvx, sendy, recvy, modes, grads, mixed, small, smalls,
    w_sem, gs_sem, sx_sem, rx_sem, sy_sem, ry_sem, ss_sem, rs_sem,
):
    d = lax.axis_index("gx")
    e = lax.axis_index("gy")

    w_copy = pltpu.make_async_copy(w_hbm, w_v, w_sem)
    w_copy.start()

    barrier = pltpu.get_barrier_semaphore()

    def greet_x(k, carry):
        pl.semaphore_signal(
            barrier, inc=1, device_id=(lax.rem(d + k, GX), e), device_id_type=MESH
        )
        return carry

    def greet_y(k, carry):
        pl.semaphore_signal(
            barrier, inc=1, device_id=(d, lax.rem(e + k, GY)), device_id_type=MESH
        )
        return carry

    lax.fori_loop(1, GX, greet_x, 0)
    lax.fori_loop(1, GY, greet_y, 0)

    def x_copy(p, peer, slot):
        return pltpu.make_async_remote_copy(
            src_ref=sendx.at[p, peer],
            dst_ref=recvx.at[p, slot],
            send_sem=sx_sem.at[p, peer],
            recv_sem=rx_sem.at[p, slot],
            device_id=(peer, e),
            device_id_type=MESH,
        )

    def y_copy(p, peer, slot):
        return pltpu.make_async_remote_copy(
            src_ref=sendy.at[p, peer],
            dst_ref=recvy.at[p, slot],
            send_sem=sy_sem.at[p, peer],
            recv_sem=ry_sem.at[p, slot],
            device_id=(d, peer),
            device_id_type=MESH,
        )

    def start_x(p):
        def go(k, carry):
            x_copy(p, lax.rem(d + k, GX), d).start()
            return carry

        lax.fori_loop(1, GX, go, 0)
        recvx[p, d] = sendx[p, d]

    def wait_x(p):
        def go(k, carry):
            peer = lax.rem(d + GX - k, GX)
            copy = x_copy(p, peer, peer)
            copy.wait_recv()
            copy.wait_send()
            return carry

        lax.fori_loop(1, GX, go, 0)

    def start_y(p):
        def go(k, carry):
            y_copy(p, lax.rem(e + k, GY), e).start()
            return carry

        lax.fori_loop(1, GY, go, 0)
        recvy[p, e] = sendy[p, e]

    def wait_y(p):
        def go(k, carry):
            peer = lax.rem(e + GY - k, GY)
            copy = y_copy(p, peer, peer)
            copy.wait_recv()
            copy.wait_send()
            return carry

        lax.fori_loop(1, GY, go, 0)

    def depth_analyse(p, get, terms):
        for t in range(XC + 1):
            total = None
            for tab, half in terms:
                if t < XC:
                    rows = get(t, half)[0:128]
                else:
                    rows = jnp.concatenate([get(x, half)[128:ROWS] for x in range(XC)], axis=0)
                term = dot(dtab[tab], rows, NTD)
                total = term if total is None else total + term
            sendx[p, :, :, t * 128 : (t + 1) * 128] = total.reshape(GX, 8, 128)

    def x_analyse(p):
        left = recvx[p, :, :, 512:640].reshape(256, 128)
        total = None
        for x in range(XC):
            tile = recvx[p, :, :, x * 128 : (x + 1) * 128].reshape(256, 128)
            tail = left if x == 0 else pltpu.roll(left, 128 - 32 * x, 1)
            term = dot3((xa[0, x], xa[1, x]), split(jnp.concatenate([tile, tail], axis=1)))
            total = term if total is None else total + term
        sendy[p] = total.reshape(GY, 32, 256)

    def y_analyse(p, out):
        rows = []
        for t, count in ((0, 16), (1, C - 16)):
            parts = [
                recvy[p, g % GY, 16 * (g // GY) : 16 * (g // GY) + 16, t * 128 : (t + 1) * 128]
                for g in range(16)
            ]
            rows += swap_groups(parts)[:count]
        out[...] = dot3(split(jnp.concatenate(rows, axis=0)), (ya[0], ya[1]))

    def y_synthesise(p):
        cols = dot3(split(mixed[...]), (ys[0], ys[1]))
        blank = jnp.zeros((16, 128), F32)
        for t, count in ((0, 16), (1, C - 16)):
            parts = [cols[(16 * t + c) * 16 : (16 * t + c + 1) * 16] for c in range(count)]
            parts = swap_groups(parts + [blank] * (16 - count))
            for g in range(16):
                sendy[
                    p, g % GY, 16 * (g // GY) : 16 * (g // GY) + 16, t * 128 : (t + 1) * 128
                ] = parts[g]

    def x_synthesise(py, px):
        cols = split(recvy[py].reshape(256, 256))
        left = None
        for x in range(XC):
            out = dot3((xs[0, x], xs[1, x]), cols)
            sendx[px, :, :, x * 128 : (x + 1) * 128] = out[:, :128].reshape(GX, 8, 128)
            tail = out[:, 128:]
            left = tail if x == 0 else left + pltpu.roll(tail, 32 * x, 1)
        sendx[px, :, :, 512:640] = left.reshape(GX, 8, 128)

    def depth_synthesise(p, x, left):
        tile = recvx[p, :, :, x * 128 : (x + 1) * 128].reshape(256, 128).T
        cols = jnp.concatenate([tile, left[32 * x : 32 * x + 32]], axis=0)
        return dot3(split(cols), (dtab[0], dtab[1])) * (1.0 / CELLS)

    def left_of(p):
        return recvx[p, :, :, 512:640].reshape(256, 128).T

    for x in range(XC):
        vb[x] = hist[:, x].astype(F32).reshape(ROWS, 512).astype(BF16)
    depth_analyse(0, lambda x, half: vb[x], ((0, 0), (1, 0)))

    pl.semaphore_wait(barrier, GX + GY - 2)
    start_x(0)

    w_copy.wait()

    def pack(o, carry):
        for r in range(2):
            for i in range(C):
                for k in range(KX):
                    wp[r, o, i, 4 * k : 4 * k + 4, 0:MY] = w_v[r, o, i, k]
        return carry

    lax.fori_loop(0, C, pack, 0)

    spread = (
        lax.broadcasted_iota(jnp.int32, (ROWS, C), 0) // YC
        == lax.broadcasted_iota(jnp.int32, (ROWS, C), 1)
    ).astype(F32)
    same_y = lax.rem(lax.broadcasted_iota(jnp.int32, (ROWS, ROWS), 0), YC) == lax.rem(
        lax.broadcasted_iota(jnp.int32, (ROWS, ROWS), 1), YC
    )
    wide = exact(exact(spread, wpt[...]), spread, NTD)
    point = split(jnp.where(same_y, wide, 0.0))
    wide_t = exact(exact(spread, wpt[...], ((1,), (1,))), spread, NTD)
    point_t = split(jnp.where(same_y, wide_t, 0.0))
    bias = jnp.sum(spread * off[...], axis=1, keepdims=True)
    for x in range(XC):
        base[x] = dot(point[0], vb[x], NN) + dot(point[1], vb[x], NN) + bias

    wait_x(0)
    x_analyse(0)
    start_y(0)
    wait_y(0)
    y_analyse(0, modes)

    valid = (lax.broadcasted_iota(jnp.int32, (16, 128), 0) < 4 * KX) & (
        lax.broadcasted_iota(jnp.int32, (16, 128), 1) < MY
    )

    def mix(o, carry):
        real = jnp.zeros((16, 128), F32)
        imag = jnp.zeros((16, 128), F32)
        for i in range(C):
            wr, wi = wp[0, o, i], wp[1, o, i]
            mr, mi = modes[16 * i : 16 * i + 16, 0:128], modes[16 * i : 16 * i + 16, 128:256]
            real += wr * mr - wi * mi
            imag += wr * mi + wi * mr
        at = pl.ds(pl.multiple_of(o * 16, 16), 16)
        mixed[at, 0:128] = jnp.where(valid, real, 0.0)
        mixed[at, 128:256] = jnp.where(valid, imag, 0.0)
        return carry

    lax.fori_loop(0, C, mix, 0)
    y_synthesise(1)
    start_y(1)
    wait_y(1)
    x_synthesise(1, 1)
    start_x(1)
    wait_x(1)

    left = left_of(1)
    row_sum = jnp.zeros((ROWS, 1), F32)
    for x in range(XC):
        pre = depth_synthesise(1, x, left) + base[x]
        inner = gelu_coef * (pre + gelu_cubic * pre * pre * pre)
        smooth = jnp.tanh(inner)
        slope = 0.5 * (1.0 + smooth) + 0.5 * pre * (1.0 - smooth * smooth) * gelu_coef * (
            1.0 + 3.0 * gelu_cubic * pre * pre
        )
        act[:, x] = (0.5 * pre * (1.0 + smooth)).reshape(C, YC, 512).astype(BF16)
        grad = cot[:, x].astype(F32).reshape(ROWS, 512) * slope
        row_sum += jnp.sum(grad, axis=1, keepdims=True)
        hi, lo = split(grad)
        gpre[0, x] = hi
        gpre[1, x] = lo
    depth_analyse(2, lambda x, half: gpre[half, x], ((0, 0), (0, 1), (1, 0)))
    start_x(2)

    cross = jnp.zeros((ROWS, ROWS), F32)
    for x in range(XC):
        g = (gpre[0, x], gpre[1, x])
        base[x] = dot3(point_t, g)
        cross += dot(g[0], vb[x], NTD) + dot(g[1], vb[x], NTD)
    gather = (
        lax.broadcasted_iota(jnp.int32, (24, ROWS), 1) // YC
        == lax.broadcasted_iota(jnp.int32, (24, ROWS), 0)
    ).astype(F32)
    place = (
        lax.broadcasted_iota(jnp.int32, (ROWS, 128), 0) // YC
        == lax.broadcasted_iota(jnp.int32, (ROWS, 128), 1)
    ).astype(F32)
    lane = lax.broadcasted_iota(jnp.int32, (ROWS, 128), 1)
    both = exact(jnp.where(same_y, cross, 0.0), place) + jnp.where(lane == C, row_sum, 0.0)
    small[0] = exact(gather, both)

    def small_copy(s, k, peer, slot):
        return pltpu.make_async_remote_copy(
            src_ref=small.at[s],
            dst_ref=smalls.at[s, slot],
            send_sem=ss_sem.at[s, k],
            recv_sem=rs_sem.at[s, slot],
            device_id=peer,
            device_id_type=MESH,
        )

    xpos, zpos = d // ZPOS, lax.rem(d, ZPOS)
    steps = (
        (GY, e, lambda i: (d, i)),
        (XPOS, xpos, lambda i: (i * ZPOS + zpos, e)),
        (ZPOS, zpos, lambda i: (xpos * ZPOS + i, e)),
    )

    def start_small(s):
        count, me, peer_of = steps[s]
        for k in range(1, count):
            small_copy(s, k, peer_of(lax.rem(me + k, count)), me).start()
        smalls[s, me] = small[s]

    def finish_small(s):
        count, me, peer_of = steps[s]
        for k in range(1, count):
            other = lax.rem(me + count - k, count)
            copy = small_copy(s, k, peer_of(other), other)
            copy.wait_recv()
            copy.wait_send()
        total = smalls[s, 0]
        for k in range(1, count):
            total = total + smalls[s, k]
        return total

    start_small(0)
    wait_x(2)
    x_analyse(2)
    start_y(2)
    small[1] = finish_small(0)
    start_small(1)
    wait_y(2)
    y_analyse(2, grads)

    def mix_back(j, carry):
        real = jnp.zeros((16, 128), F32)
        imag = jnp.zeros((16, 128), F32)
        for o in range(C):
            wr, wi = wp[0, o, j], wp[1, o, j]
            gr, gi = grads[16 * o : 16 * o + 16, 0:128], grads[16 * o : 16 * o + 16, 128:256]
            real += wr * gr + wi * gi
            imag += wr * gi - wi * gr
        at = pl.ds(pl.multiple_of(j * 16, 16), 16)
        mixed[at, 0:128] = jnp.where(valid, real, 0.0)
        mixed[at, 128:256] = jnp.where(valid, imag, 0.0)
        return carry

    lax.fori_loop(0, C, mix_back, 0)
    y_synthesise(3)
    start_y(3)
    small[2] = finish_small(1)
    start_small(2)
    wait_y(3)
    x_synthesise(3, 3)
    start_x(3)

    def pair(o, carry):
        at = pl.ds(pl.multiple_of(o * 16, 16), 16)
        gr = grads[at, 0:128] * (1.0 / CELLS)
        gi = grads[at, 128:256] * (1.0 / CELLS)
        for j in range(C):
            mr, mi = modes[16 * j : 16 * j + 16, 0:128], modes[16 * j : 16 * j + 16, 128:256]
            real = gr * mr + gi * mi
            imag = gi * mr - gr * mi
            for k in range(KX):
                gs_v[0, o, j, k] = real[4 * k : 4 * k + 4, 0:MY]
                gs_v[1, o, j, k] = imag[4 * k : 4 * k + 4, 0:MY]
        return carry

    lax.fori_loop(0, C, pair, 0)
    gs_copy = pltpu.make_async_copy(gs_v, gs_hbm, gs_sem)
    gs_copy.start()

    total = finish_small(2)
    gpoint[...] = total[0:C, 0:C]
    column = total[0:C, C : C + 1]
    diagonal = lax.broadcasted_iota(jnp.int32, (C, C), 0) == lax.broadcasted_iota(
        jnp.int32, (C, C), 1
    )
    goff[...] = jnp.sum(jnp.where(diagonal, column, 0.0), axis=0, keepdims=True)

    wait_x(3)
    left = left_of(3)
    for x in range(XC):
        total = depth_synthesise(3, x, left) + base[x]
        ghist[:, x] = total.reshape(C, YC, 512).astype(BF16)
    gs_copy.wait()


def per_device(history, w_point, offset, spectral_weight, cotangent):
    depth = jnp.asarray(halves(depth_table()))
    xt = x_table()
    x_forward = jnp.asarray(halves(xt.transpose(0, 2, 1)))
    x_backward = jnp.asarray(halves(xt))
    yt = y_table()
    y_forward = jnp.asarray(halves(yt))
    y_backward = jnp.asarray(halves(yt.T))
    weight = jnp.transpose(spectral_weight, (0, 1, 2, 4, 3, 5))
    vmem = pl.BlockSpec(memory_space=pltpu.VMEM)
    hbm = pl.BlockSpec(memory_space=pl.ANY)
    block = (C, XC, YC, NZ * NT)
    act, ghist, gs, gpoint, goff = pl.pallas_call(
        kernel,
        out_shape=(
            jax.ShapeDtypeStruct(block, BF16),
            jax.ShapeDtypeStruct(block, BF16),
            jax.ShapeDtypeStruct((2, C, C, KX, Q, MY), F32),
            jax.ShapeDtypeStruct((C, C), F32),
            jax.ShapeDtypeStruct((1, C), F32),
        ),
        in_specs=[vmem] * 4 + [hbm] + [vmem] * 5,
        out_specs=(vmem, vmem, hbm, vmem, vmem),
        scratch_shapes=[
            pltpu.VMEM((2, C, C, KX, Q, MY), F32),
            pltpu.VMEM((2, C, C, 16, 128), F32),
            pltpu.VMEM((2, C, C, KX, Q, MY), F32),
            pltpu.VMEM((XC, ROWS, 512), BF16),
            pltpu.VMEM((XC, ROWS, 512), F32),
            pltpu.VMEM((2, XC, ROWS, 512), BF16),
            pltpu.VMEM((4, GX, 8, 640), F32),
            pltpu.VMEM((4, GX, 8, 640), F32),
            pltpu.VMEM((4, GY, 32, 256), F32),
            pltpu.VMEM((4, GY, 32, 256), F32),
            pltpu.VMEM((C * 16, 256), F32),
            pltpu.VMEM((C * 16, 256), F32),
            pltpu.VMEM((C * 16, 256), F32),
            pltpu.VMEM((3, 24, 128), F32),
            pltpu.VMEM((3, 8, 24, 128), F32),
            pltpu.SemaphoreType.DMA,
            pltpu.SemaphoreType.DMA,
            pltpu.SemaphoreType.DMA((4, GX)),
            pltpu.SemaphoreType.DMA((4, GX)),
            pltpu.SemaphoreType.DMA((4, GY)),
            pltpu.SemaphoreType.DMA((4, GY)),
            pltpu.SemaphoreType.DMA((3, 8)),
            pltpu.SemaphoreType.DMA((3, 8)),
        ],
        compiler_params=pltpu.CompilerParams(
            collective_id=0, has_side_effects=True, vmem_limit_bytes=58 * 1024 * 1024
        ),
    )(
        history[0], cotangent[0], w_point, offset.reshape(1, C), weight,
        depth, x_forward, x_backward, y_forward, y_backward,
    )
    grad_spectral = jnp.transpose(gs, (0, 1, 2, 4, 3, 5))
    return act[None], ghist[None], grad_spectral, gpoint, goff.reshape(C)


def solution(mesh):
    grid = P(None, None, "gx", "gy", None)
    modes = P(None, None, None, "gx", "gy", None)
    return jax.shard_map(
        per_device,
        mesh=mesh,
        in_specs=(grid, P(), P(), modes, grid),
        out_specs=(grid, grid, modes, P(), P()),
        check_vma=False,
    )
```

time: 573 us -> 131 us (0.23); the launches traced: 563 us -> 130 us
  blocking collectives: 136 us -> 0 us
  Pallas kernels: 0 us -> 119 us
  matrix products: 107 us -> 0 us
  local copies, waits for them, and re-layouts: 104 us -> 10.6 us
  waiting for transfers between devices: 77.2 us -> 0 us
  starting transfers between devices: 72.3 us -> 0 us
  other arithmetic: 50.6 us -> 0 us
  between operations: 16.1 us -> 0.64 us
    pallas_call x0 -> x1, Pallas kernels: none -> 119 us  [per_device(): pl.pallas_call(kernel, out_shape=(jax.ShapeDtypeStruct(block, BF16), jax....]
    dot_general x43 -> x0, matrix products: 107 us -> none  [the longest x35 88.9 us: contract(): return jnp.einsum(form, left, right, precision=lax.Precision.HIGHEST)]
    psum x1 -> x0, blocking collectives: 77.5 us -> none  [per_device(): lax.psum((local_point, local_offset), ('gx', 'gy'))]
    all_to_all x8 -> x0, starting transfers between devices: 71.7 us -> none  [the longest x2 21.2 us: analyse(): lax.all_to_all(depth_imag, 'gx', split_axis=4, concat_axis=2, tiled=True)]
    unnamed x4 -> x0, waiting for transfers between devices: 67.8 us -> none
    all_gather x4 -> x0, blocking collectives: 58.6 us -> none  [the longest x2 30.5 us: synthesise(): lax.all_gather(spec_real, 'gy', axis=2, tiled=True)]
    unnamed x69 -> x9, local copies, waits for them, and re-layouts: 52.5 us -> 10.6 us
    another operation x16 -> x0, local copies, waits for them, and re-layouts: 17.9 us -> none
  transfers between devices with their start and end apart: 10 -> 0, of which waited for: 6 -> 0; matrix products, arithmetic and copies ran while one was open for 14% -> 0% of each run, Pallas kernels for 0% -> 0%
where the time goes in v1:
time: 131 us; the launch traced here: 130 us
  Pallas kernels  119 us (91%)
  local copies, waits for them, and re-layouts  10.6 us (8%)
    pallas_call x1, Pallas kernels, per_device(): pl.pallas_call(kernel, out_shape=(jax.ShapeDtypeStruct(block, BF16), jax....  119 us
    unnamed x9, local copies, waits for them, and re-layouts  10.6 us

profile of v1, /device:TPU:1, one launch (start us, length us, event | category | flops | bytes accessed | tf_op | source)
XLA Modules:
  0.0 130.5 jit_solution(5751298988872692118)
XLA Ops:
  0.6 119.3 %shard_map.137 = (bf16[20,4,8,512]{3,2,1,0:T(8,128)(2,1)}, bf16[20,4,8,512]{3,2,1,0:T(8,128)(2,1)}, f32[2,20,20,3,4,24]{5,4,3,2,1,0:T(4,128)}, f32[20,20]{1,0:T(8,128)}, f32[1,20]{1,0:T(1,128)}) custom-call(bf16[20,4,8,512]{3,2,1,0:T(8,128)(2,1)} %bitcast.10, bf16[20,4,8,512]{3,2,1,0:T(8,128)(2,1)} %bitcast.11, f32[20,20]{1,0:T(8,128)} %wpt.1, ...), custom_call_target="tpu_custom_call" | custom-call | tf_op jit(solution)/shard_map/pallas_call | solution.py:471
  119.9 2.0 %copy.20 = bf16[1,20,4,8,512]{4,3,2,1,0:T(8,128)(2,1)} copy(bf16[1,20,4,8,512]{4,3,2,1,0:T(8,128)(2,1)} %bitcast.13) | data formatting | bytes 1310720
  121.9 2.0 %copy.21 = bf16[1,20,4,8,512]{4,3,2,1,0:T(8,128)(2,1)} copy(bf16[1,20,4,8,512]{4,3,2,1,0:T(8,128)(2,1)} %bitcast.12) | data formatting | bytes 1310720
  123.9 0.0 copy-start
  123.9 0.0 copy-start.1
  123.9 5.5 %copy.22 = f32[2,20,20,4,3,24]{5,3,4,2,1,0:T(4,128)} copy(f32[2,20,20,4,3,24]{5,3,4,2,1,0:T(4,128)} %bitcast.9) | data formatting | bytes 1843200
  129.4 0.0 copy-done
  129.4 0.6 copy.23
  130.0 0.0 copy-done.1
  130.0 0.5 copy.24
Async XLA Ops:
  123.9 5.5 %copy-start = (f32[20,20]{1,0:T(8,128)S(1)}, f32[20,20]{1,0:T(8,128)}, u32[]{:S(2)}) copy-start(f32[20,20]{1,0:T(8,128)} %get-tuple-element.23) | copy-start | bytes 4804
  123.9 6.1 %copy-start.1 = (f32[1,20]{1,0:T(1,128)S(1)}, f32[1,20]{1,0:T(1,128)}, u32[]{:S(2)}) copy-start(f32[1,20]{1,0:T(1,128)} %get-tuple-element.14) | copy-start | bytes 244

commit v2 on v1

v2 whole, which is shorter than its diff:
```python
import functools

import jax
import jax.numpy as jnp
import ml_dtypes
import numpy as np
from jax import lax
from jax.experimental import pallas as pl
from jax.experimental.pallas import tpu as pltpu
from jax.sharding import PartitionSpec as P

MESH = pl.DeviceIdType.MESH
F32 = jnp.float32
BF16 = jnp.bfloat16
C = 20
NX, NY, NZ, NT = 128, 64, 64, 8
MX, MY, MZ, MT = 24, 24, 16, 8
GX, GY = 32, 8
XC, YC = NX // GX, NY // GY
KX = MX // GY
Q = MZ * MT // GX
ROWS = C * YC
CELLS = NX * NY * NZ * NT
XPOS, ZPOS = 4, 8
EXTRA, STRIDE = 4, 10
gelu_coef = 0.7978845608028654
gelu_cubic = 0.044715


def kept(length, keep):
    half = keep // 2
    return np.concatenate([np.arange(half), length - half + np.arange(half)])


def halves(table):
    table = np.asarray(table, np.float64)
    hi = table.astype(np.float32).astype(ml_dtypes.bfloat16)
    lo = (table - hi.astype(np.float64)).astype(np.float32).astype(ml_dtypes.bfloat16)
    return np.stack([hi, lo])


def handled(h):
    p, s = h // 2, h % 2
    if p == 0:
        return [(NZ - 8, t) for t in ((2, 3) if s == 0 else (6, 7))]
    if p == 8:
        return [(NZ - 8, t) for t in ((0, 1) if s == 0 else (4, 5))]
    if p < 8:
        return [(p, t) for t in ((0, 3) if s == 0 else (4, 7))]
    return [(16 - p, t) for t in ((5, 6) if s == 0 else (1, 2))]


def depth_table():
    z, t = np.arange(NZ)[:, None], np.arange(NT)[None]

    def wave(kz, kt):
        return 2 * np.pi * ((z * kz % NZ) / NZ + (t * kt % NT) / NT).reshape(-1)

    rows = []
    for h in range(GX):
        angles = [wave(*mode) for mode in handled(h)]
        rows += [np.cos(a) for a in angles] + [-np.sin(a) for a in angles]
    rows += [np.cos(wave(0, 0)), np.cos(wave(0, 4))]
    for j in range(1, EXTRA):
        rows += [np.cos(wave(0, j)), -np.sin(wave(0, j))]
    return np.stack(rows + [np.zeros(NZ * NT)] * 8)


def x_tables():
    fx = kept(NX, MX).reshape(GY, KX)
    x = np.arange(NX).reshape(GX, XC).T
    angle = 2 * np.pi * (fx[:, :, None, None] * x[None, None] % NX) / NX
    cos, sin = np.cos(angle), np.sin(angle)
    main = np.zeros((GY, 2, 16, XC, GX, 2, 2))
    extra = np.zeros((2, GY, 2, 16, XC, GX, 2))
    direct = ((cos, sin), (-sin, cos))
    conj = ((cos, -sin), (-sin, -cos))
    for out in range(2):
        for k in range(KX):
            row = 6 * out + 2 * k
            for into in range(2):
                for m in range(2):
                    main[:, 0, row + m, :, :, into, m] = direct[out][into][:, k]
                    main[:, 1, row + m, :, :, into, m] = conj[out][into][:, k]
                extra[1, :, 0, row, :, :, into] = direct[out][into][:, k]
                extra[1, :, 1, row, :, :, into] = conj[out][into][:, k]
            extra[0, :, 0, row, :, :, 0] = direct[out][0][:, k]
            extra[0, :, 1, row, :, :, 1] = direct[out][0][:, k]

    def spread_rows(full):
        out = np.zeros((4,) + full.shape[:2] + (4,) + full.shape[3:])
        for g in range(4):
            out[g, :, :, :3] = full[:, :, g:12:4]
        return out

    def both(full):
        tail = spread_rows(full)
        columns = full[0, 0, 0].size
        rows = tail.transpose(0, 2, 1, *range(3, tail.ndim))
        return (
            full.reshape(256, columns),
            tail.reshape(256, columns),
            full.swapaxes(0, 1).reshape(2, GY * 16, columns),
            rows.reshape(4, 2, GY * 4, columns),
        )

    am, al, sm, sl = both(main)
    sm = np.concatenate([sm[0], sm[1], sm[1]]).T
    sl = np.concatenate([sl[:, :1], sl[:, 1:], sl[:, 1:]], axis=1).reshape(384, -1).T
    ex = [both(extra[kind]) for kind in range(2)]
    em, el = np.stack([v[0] for v in ex]), np.stack([v[1] for v in ex])
    esm = np.stack([v[2].reshape(256, 256).T for v in ex])
    esl = np.stack([v[3].reshape(256, 256).T for v in ex])
    return np.stack([am, al]), np.stack([sm, sl]), np.stack([em, el, esm, esl], axis=1)


def slot_tables():
    maps = (
        {(0, 0): 0, (0, 1): 3, (1, 0): 1, (1, 1): 2},
        {(0, 0): 3, (0, 1): 2, (1, 0): 0, (2, 1): 1},
        {(0, 0): 3, (0, 1): 2, (1, 1): 1, (2, 0): 0},
        {(0, 0): 0, (0, 1): 1, (1, 0): 2, (1, 1): 3},
        {(0, 0): 0, (1, 0): 1, (2, 0): 2, (3, 0): 3},
        {(0, 0): 0, (1, 0): 3, (2, 0): 2, (3, 0): 1},
    )
    out = np.zeros((len(maps), 64, 160))
    for kind, table in enumerate(maps):
        for (slot, m), q in table.items():
            for ri in range(2):
                for k in range(KX):
                    r = 6 * ri + 2 * k + m
                    at = 16 * ri + 4 * k + q
                    out[kind, 16 * slot + r, at] = 1
                    out[kind, 16 * slot + 12 + r // 4, 32 + 32 * (r % 4) + at] = 1
    return out


def y_table():
    fy = kept(NY, MY)
    angle = 2 * np.pi * (np.arange(NY)[:, None] * fy[None] % NY) / NY
    cos, sin = np.cos(angle), np.sin(angle)
    out = np.zeros((2, NY, 2, 128))
    out[0, :, 0, :MY] = cos
    out[1, :, 0, :MY] = sin
    out[0, :, 1, :MY] = -sin
    out[1, :, 1, :MY] = cos
    return out.reshape(2 * NY, 256)


def split(value):
    hi = value.astype(BF16)
    return hi, (value - hi.astype(F32)).astype(BF16)


def dot(a, b, dims):
    return lax.dot_general(a, b, (dims, ((), ())), preferred_element_type=F32)


NN = ((1,), (0,))
NTD = ((1,), (1,))


def dot3(a, b, dims=NN):
    return dot(a[0], b[0], dims) + (dot(a[0], b[1], dims) + dot(a[1], b[0], dims))


def exact(a, b, dims=NN):
    return lax.dot_general(
        a, b, (dims, ((), ())), precision=lax.Precision.HIGHEST, preferred_element_type=F32
    )


def swap_groups(parts):
    parts = list(parts)
    group = lax.broadcasted_iota(jnp.int32, parts[0].shape, 1) // 8
    for s in (8, 4, 2, 1):
        low = lax.rem(group // s, 2) == 0
        for i in range(16):
            if i & s:
                continue
            a, b = parts[i], parts[i + s]
            parts[i] = jnp.where(low, a, pltpu.roll(b, 8 * s, 1))
            parts[i + s] = jnp.where(low, pltpu.roll(a, 128 - 8 * s, 1), b)
    return parts


def dot2(a, b):
    return dot(a, b[0], NN) + dot(a, b[1], NN)


def kernel(
    hist, cot, wpt, off, w_hbm, dtab_h, xa_h, xs_h, xe_h, ya_h, ys_h, u_h, ut_h,
    fields, sums,
    dtab, xa, xs, xe, ya, ys, u, ut, w_v, wp, vb, base, gpre, mixed,
    sendx, recvx, sende, recve, sendr, recvr, sendy, recvy, backs, backr, exy, small, smalls,
    load_sem, sx_sem, rx_sem, se_sem, re_sem, sr_sem, rr_sem, sy_sem, ry_sem, sb_sem, rb_sem, ss_sem, rs_sem,
):
    d = lax.axis_index("gx")
    e = lax.axis_index("gy")
    modes, grads = sums.at[0:320], sums.at[320:640]
    half, side = d // 2, lax.rem(d, 2)
    is_a = (d >= 2) & (d < 16)
    is_b = d >= 18
    is_mid = (d >= 16) & (d < 18)
    is_low = d < 2
    special = lax.rem(d, STRIDE) == 0
    which = d // STRIDE
    kind = jnp.where(is_low, 4 + side, jnp.where(is_mid, 3, jnp.where(is_a, 0, 1 + side)))
    kind_e = jnp.where(d == 0, 0, 1)
    pair = GX - 2 * half
    mirror = GX + 1 - d

    loads = [
        pltpu.make_async_copy(src, dst, load_sem.at[i])
        for i, (src, dst) in enumerate((
            (dtab_h, dtab), (w_hbm, w_v), (xa_h, xa), (xs_h, xs), (ya_h, ya), (ys_h, ys),
            (u_h.at[kind], u), (ut_h.at[kind], ut),
        ))
    ]
    extra_load = pltpu.make_async_copy(xe_h.at[:, kind_e], xe, load_sem.at[len(loads)])
    for load in loads:
        load.start()

    @pl.when(special)
    def _():
        extra_load.start()

    recvy[...] = jnp.zeros_like(recvy)
    backr[...] = jnp.zeros_like(backr)

    barrier = pltpu.get_barrier_semaphore()

    def signal(x, y):
        pl.semaphore_signal(barrier, inc=1, device_id=(x, y), device_id_type=MESH)

    def over(count, body, first=0):
        def go(k, carry):
            body(k)
            return carry

        lax.fori_loop(first, count, go, 0)

    over(GX, lambda k: signal((d + k) & (GX - 1), e), 1)
    over(GY, lambda k: signal(d, (e + k) & (GY - 1)), 1)
    def remote(src, dst, send, recv, x, y):
        return pltpu.make_async_remote_copy(
            src_ref=src, dst_ref=dst, send_sem=send, recv_sem=recv,
            device_id=(x, y), device_id_type=MESH,
        )

    def x_copy(p, peer, slot):
        return remote(
            sendx.at[p, peer], recvx.at[p, slot], sx_sem.at[p, peer], rx_sem.at[p, slot], peer, e
        )

    def start_x(p):
        over(GX, lambda k: x_copy(p, (d + k) & (GX - 1), d).start(), 1)
        recvx[p, d] = sendx[p, d]

    def wait_x(p):
        def go(k):
            peer = (d + GX - k) & (GX - 1)
            copy = x_copy(p, peer, peer)
            copy.wait_recv()
            copy.wait_send()

        over(GX, go, 1)

    def e_copy(f, j, slot):
        return remote(
            sende.at[f, j], recve.at[f, slot], se_sem.at[f, j], re_sem.at[f, slot], j * STRIDE, e
        )

    def start_e(f):
        def go(j):
            @pl.when(d != j * STRIDE)
            def _():
                e_copy(f, j, d).start()

        over(EXTRA, go)

        @pl.when(special)
        def _():
            recve[f, d] = sende[f, which]

    def wait_e_sent(f):
        def go(j):
            @pl.when(d != j * STRIDE)
            def _():
                e_copy(f, j, d).wait_send()

        over(EXTRA, go)

    def wait_e(f):
        def go(k):
            peer = (d + GX - k) & (GX - 1)
            remote(
                sende.at[f, 0], recve.at[f, peer], se_sem.at[f, 0], re_sem.at[f, peer], peer, e
            ).wait_recv()

        over(GX, go, 1)

    def r_copy(f, peer, j):
        return remote(
            sendr.at[f, peer], recvr.at[f, j], sr_sem.at[f, peer], rr_sem.at[f, j], peer, e
        )

    def start_r(f):
        over(GX, lambda k: r_copy(f, (d + k) & (GX - 1), which).start(), 1)
        recvr[f, which] = sendr[f, d]

    def wait_r(f):
        def go(j):
            @pl.when(d != j * STRIDE)
            def _():
                r_copy(f, 0, j).wait_recv()

        over(EXTRA, go)

        @pl.when(special)
        def _():
            over(GX, lambda k: r_copy(f, (d + k) & (GX - 1), which).wait_send(), 1)

    others = jnp.where(is_a, 2, jnp.where(is_mid, 0, 1))
    own_part = jnp.where(is_b, 1, 0)
    other_part = jnp.where(is_a, 1, 0)
    other_slot = jnp.where(is_a, 1 + side, 1)

    def other_at(t):
        return jnp.where(is_a, pair + t, jnp.where(is_low, d + 16, mirror))

    def y_copy(f, y, part, slot, x, sem):
        return remote(
            sendy.at[f, y, part], recvy.at[f, slot, e], sy_sem.at[f, sem, y], ry_sem.at[f, slot, e], x, y
        )

    def ex_copy(f, y, part):
        return remote(
            exy.at[f, y, part], recvy.at[f, which, e], sy_sem.at[f, 3 + part, y],
            ry_sem.at[f, which, e], part, y,
        )

    def each_y(f, act_on):
        def own(k):
            y = (e + k) & (GY - 1)
            act_on(y_copy(f, y, own_part, 0, d, 0))

        @pl.when(d >= 2)
        def _():
            over(GY, own, 1)

        def other(k):
            y = (e + k) & (GY - 1)
            over(
                others,
                lambda t: act_on(y_copy(f, y, other_part, other_slot, other_at(t), 1 + t)),
            )

        over(GY, other)

    def each_ex(f, act_on):
        def go(k):
            y = (e + k) & (GY - 1)

            @pl.when((d != 0) | (k != 0))
            def _():
                act_on(ex_copy(f, y, 0))

            act_on(ex_copy(f, y, 1))

        over(GY, go)

    def start_y(f):
        each_y(f, lambda copy: copy.start())

        @pl.when(d >= 2)
        def _():
            recvy[f, 0, e] = sendy[f, e, own_part]

    def start_ex(f):
        each_ex(f, lambda copy: copy.start())

        @pl.when(d == 0)
        def _():
            recvy[f, 0, e] = exy[f, e, 0]

    def wait_y(f):
        def arrived(slot, y):
            remote(
                sendy.at[f, 0, 0], recvy.at[f, slot, y], sy_sem.at[f, 0, 0], ry_sem.at[f, slot, y], d, y
            ).wait_recv()

        @pl.when(d >= 1)
        def _():
            over(GY, lambda k: arrived(0, (e + GY - k) & (GY - 1)), 1)

        @pl.when(d == 1)
        def _():
            arrived(0, e)

        @pl.when(d == 0)
        def _():
            over(GY, lambda k: arrived(0, (e + GY - k) & (GY - 1)), 1)

        slots = jnp.where(is_low, 4, jnp.where(is_b, 3, 2))

        def rest(k):
            y = (e + GY - k) & (GY - 1)
            over(slots, lambda slot: arrived(slot, y), 1)

        over(GY, rest)
        each_y(f, lambda copy: copy.wait_send())

        @pl.when(special)
        def _():
            each_ex(f, lambda copy: copy.wait_send())

    def b_copy(f, slot, y, x, into):
        return remote(
            backs.at[f, slot, y], backr.at[f, into, e], sb_sem.at[f, slot, y], rb_sem.at[f, into, e], x, y
        )

    def each_b(f, act_on):
        def own(k):
            y = (e + k) & (GY - 1)
            act_on(b_copy(f, 0, y, d, jnp.where(is_b, 1, 0)))

        @pl.when(d >= 2)
        def _():
            over(GY, own, 1)

        def other(k):
            y = (e + k) & (GY - 1)

            @pl.when(is_a | is_mid)
            def _():
                act_on(b_copy(f, 1, y, jnp.where(is_a, mirror, d - 16), 0))

            @pl.when(is_b)
            def _():
                over(2, lambda t: act_on(b_copy(f, 1 + t, y, pair + t, 1 + side)))

            @pl.when(is_low)
            def _():
                def slot(j):
                    @pl.when((d != 0) | (j != 0) | (k != 0))
                    def _():
                        act_on(b_copy(f, j, y, j * STRIDE, 3 + side))

                over(EXTRA, slot)

        over(GY, other)

    def start_b(f):
        each_b(f, lambda copy: copy.start())

        @pl.when(d >= 2)
        def _():
            backr[f, jnp.where(is_b, 1, 0), e] = backs[f, 0, e]

        @pl.when(d == 0)
        def _():
            backr[f, 3, e] = backs[f, 0, e]

    def wait_b(f):
        def arrived(into, y):
            remote(
                backs.at[f, 0, 0], backr.at[f, into, y], sb_sem.at[f, 0, 0], rb_sem.at[f, into, y], d, y
            ).wait_recv()

        def own(k):
            arrived(jnp.where(is_b, 1, 0), (e + GY - k) & (GY - 1))

        @pl.when(d >= 2)
        def _():
            over(GY, own, 1)

        def rest(k):
            y = (e + GY - k) & (GY - 1)

            @pl.when(is_a)
            def _():
                over(3, lambda into: arrived(into, y), 1)

            @pl.when(is_b | is_low)
            def _():
                arrived(0, y)

        over(GY, rest)
        each_b(f, lambda copy: copy.wait_send())

    def wait_b_extra(f):
        def go(k):
            y = (e + GY - k) & (GY - 1)

            @pl.when((d != 0) | (k != 0))
            def _():
                remote(
                    backs.at[f, 0, 0], backr.at[f, 3, y], sb_sem.at[f, 0, 0], rb_sem.at[f, 3, y], d, y
                ).wait_recv()

            remote(
                backs.at[f, 0, 0], backr.at[f, 4, y], sb_sem.at[f, 0, 0], rb_sem.at[f, 4, y], d, y
            ).wait_recv()

        over(GY, go)

    lane128 = lax.broadcasted_iota(jnp.int32, (1, 128), 1)

    def depth_analyse(p, f, get, terms):
        for t in range(XC + 1):
            total = None
            for tab, part in terms:
                if t < XC:
                    rows = get(t, part)[0:128]
                else:
                    rows = jnp.concatenate([get(x, part)[128:ROWS] for x in range(XC)], axis=0)
                term = dot(dtab[tab], rows, NTD)
                total = term if total is None else total + term
            sendx[p, :, t] = total[0:128].reshape(GX, 4, 128)
            sende[f, :, t] = total[128:136].reshape(EXTRA, 2, 128)

    def x_analyse(tiles, tables, out):
        left = tiles[XC]
        count = left.shape[0]
        per = 256 // count
        main, tail = None, None
        for b in range(XC // per):
            xs_here = range(b * per, (b + 1) * per)
            at = slice(b * 256, (b + 1) * 256)
            cols = split(jnp.concatenate([tiles[x] for x in xs_here], axis=0))
            term = dot3((tables[0, 0, :, at], tables[1, 0, :, at]), cols)
            main = term if main is None else main + term
            cols = split(jnp.concatenate(
                [left if x == 0 else pltpu.roll(left, 128 - 32 * x, 1) for x in xs_here], axis=0
            ))
            term = dot3((tables[0, 1, :, at], tables[1, 1, :, at]), cols)
            tail = term if tail is None else tail + term
        out[...] = main.reshape(GY, 2, 16, 128)
        tail = jnp.where(lane128 < 32, tail, 0.0)
        packed = tail[0:64]
        for g in range(1, 4):
            packed = packed + pltpu.roll(tail[64 * g : 64 * g + 64], 32 * g, 1)
        out[:, :, 12:16, :] = packed.reshape(GY, 2, 4, 128)

    def analyse_main(p, f):
        x_analyse([recvx[p, :, t].reshape(128, 128) for t in range(XC + 1)], xa, sendy.at[f])

    def analyse_extra(f):
        x_analyse(
            [recve[f, :, t].reshape(64, 128) for t in range(XC + 1)], xe.at[:, 0:2], exy.at[f]
        )

    def y_analyse(f, out):
        cols = split(jnp.concatenate([recvy[f, :, y].reshape(64, 128) for y in range(GY)], axis=1))
        merged = dot2(ut[...], cols)
        rows = []
        parts = [
            merged[16 * (g // GY) : 16 * (g // GY) + 16, 128 * (g % GY) : 128 * (g % GY) + 128]
            for g in range(16)
        ]
        rows += swap_groups(parts)
        parts = []
        for g in range(16):
            at = 32 + 16 * (g // GY)
            lanes = slice(128 * (g % GY), 128 * (g % GY) + 128)
            total = merged[at : at + 16, lanes]
            for n in range(1, 4):
                total = total + pltpu.roll(merged[at + 32 * n : at + 32 * n + 16, lanes], 128 - 32 * n, 1)
            parts.append(total)
        rows += swap_groups([jnp.where(lane128 < 32, part, 0.0) for part in parts])[: C - 16]
        out[...] = dot3(split(jnp.concatenate(rows, axis=0)), (ya[0], ya[1]))

    def y_synthesise(f):
        cols = dot3(split(mixed[...]), (ys[0], ys[1]))
        blank = jnp.zeros((16, 128), F32)
        main = swap_groups([cols[16 * c : 16 * c + 16] for c in range(16)])
        tail = swap_groups(
            [cols[16 * c : 16 * c + 16] for c in range(16, C)] + [blank] * (32 - C)
        )
        stack = []
        for y in range(GY):
            rows = [main[y], main[GY + y]]
            for n in range(4):
                for g in (y, GY + y):
                    rows.append(tail[g] if n == 0 else pltpu.roll(tail[g], 32 * n, 1))
            stack.append(jnp.concatenate(rows, axis=0))
        out = dot2(u[...], split(jnp.concatenate(stack, axis=1)))
        for y in range(GY):
            backs[f, :, y] = out[:, 128 * y : 128 * y + 128].reshape(4, 16, 128)

    def x_synthesise(slots, tables, put):
        count = slots.shape[0] * GY
        rows = slots[...]
        main_cols = split(rows.reshape(count * 16, 128))
        tail = rows[:, :, 12:16, :].reshape(count * 4, 128)
        tail_cols = split(jnp.concatenate(
            [tail] + [pltpu.roll(tail, 128 - 32 * g, 1) for g in range(1, 4)], axis=0
        ))
        main = dot3((tables[0, 0], tables[1, 0]), main_cols)
        tail = dot3((tables[0, 1], tables[1, 1]), tail_cols)
        tail = jnp.where(lane128 < 32, tail, 0.0)
        per = main.shape[0] // XC
        left = None
        for x in range(XC):
            at = slice(per * x, per * x + per)
            put(x, main[at])
            part = tail[at]
            left = part if x == 0 else left + pltpu.roll(part, 32 * x, 1)
        put(XC, left)

    def synthesise_main(f, p):
        def put(t, rows):
            sendx[p, :, t] = rows.reshape(GX, 4, 128)

        x_synthesise(backr.at[f, 0:3], xs, put)

    def synthesise_extra(f):
        def put(t, rows):
            sendr[f, :, t] = rows.reshape(GX, 2, 128)

        x_synthesise(backr.at[f, 3:5], xe.at[:, 2:4], put)

    def depth_rows(p, f, t):
        tile = recvx[p, :, t].reshape(128, 128)
        extra = recvr[f, :, t].reshape(8, 128)
        rest = jnp.zeros((120, 128), F32)
        low = jnp.concatenate([extra, rest], axis=0).T
        return jnp.concatenate([tile.T, low[:, 0:16]], axis=1)

    def depth_synthesise(p, f, x, left):
        cols = jnp.concatenate([depth_rows(p, f, x), left[32 * x : 32 * x + 32]], axis=0)
        return dot3(split(cols), (dtab[0], dtab[1])) * (1.0 / CELLS)

    def send_main_then_extra(p, f):
        @pl.when(special)
        def _():
            wait_e(f)
            analyse_extra(f)
            start_ex(f)

        wait_x(p)
        analyse_main(p, f)
        start_y(f)

    def cells_back(f, p):
        @pl.when(special)
        def _():
            wait_b_extra(f)
            synthesise_extra(f)
            start_r(f)

        wait_b(f)
        synthesise_main(f, p)
        start_x(p)

    for x in range(XC):
        vb[x] = hist[:, x].astype(F32).reshape(ROWS, 512).astype(BF16)
    loads[0].wait()
    depth_analyse(0, 0, lambda x, part: vb[x], ((0, 0), (1, 0)))

    pl.semaphore_wait(barrier, GX + GY - 2)
    start_e(0)
    start_x(0)

    for load in loads[1:]:
        load.wait()

    @pl.when(special)
    def _():
        extra_load.wait()

    def pack(o):
        for r in range(2):
            for i in range(C):
                for k in range(KX):
                    wp[r, o, i, 4 * k : 4 * k + 4, 0:MY] = w_v[r, o, i, k]

    over(C, pack)

    spread = (
        lax.broadcasted_iota(jnp.int32, (ROWS, C), 0) // YC
        == lax.broadcasted_iota(jnp.int32, (ROWS, C), 1)
    ).astype(F32)
    same_y = lax.rem(lax.broadcasted_iota(jnp.int32, (ROWS, ROWS), 0), YC) == lax.rem(
        lax.broadcasted_iota(jnp.int32, (ROWS, ROWS), 1), YC
    )
    wide = exact(exact(spread, wpt[...]), spread, NTD)
    point = split(jnp.where(same_y, wide, 0.0))
    wide_t = exact(exact(spread, wpt[...], ((1,), (1,))), spread, NTD)
    point_t = split(jnp.where(same_y, wide_t, 0.0))
    bias = jnp.sum(spread * off[...], axis=1, keepdims=True)
    for x in range(XC):
        base[x] = dot(point[0], vb[x], NN) + dot(point[1], vb[x], NN) + bias

    send_main_then_extra(0, 0)
    wait_y(0)
    y_analyse(0, modes)

    valid = (lax.broadcasted_iota(jnp.int32, (16, 128), 0) < 4 * KX) & (
        lax.broadcasted_iota(jnp.int32, (16, 128), 1) < MY
    )

    def mix(o):
        real = jnp.zeros((16, 128), F32)
        imag = jnp.zeros((16, 128), F32)
        for i in range(C):
            wr, wi = wp[0, o, i], wp[1, o, i]
            mr, mi = modes[16 * i : 16 * i + 16, 0:128], modes[16 * i : 16 * i + 16, 128:256]
            real += wr * mr - wi * mi
            imag += wr * mi + wi * mr
        at = pl.ds(pl.multiple_of(o * 16, 16), 16)
        mixed[at, 0:128] = jnp.where(valid, real, 0.0)
        mixed[at, 128:256] = jnp.where(valid, imag, 0.0)

    over(C, mix)
    y_synthesise(0)
    start_b(0)
    cells_back(0, 1)
    wait_x(1)
    wait_r(0)
    wait_e_sent(0)

    left = depth_rows(1, 0, XC)
    row_sum = jnp.zeros((ROWS, 1), F32)
    for x in range(XC):
        pre = depth_synthesise(1, 0, x, left) + base[x]
        inner = gelu_coef * (pre + gelu_cubic * pre * pre * pre)
        smooth = jnp.tanh(inner)
        slope = 0.5 * (1.0 + smooth) + 0.5 * pre * (1.0 - smooth * smooth) * gelu_coef * (
            1.0 + 3.0 * gelu_cubic * pre * pre
        )
        fields[0, :, x] = (0.5 * pre * (1.0 + smooth)).reshape(C, YC, 512).astype(BF16)
        grad = cot[:, x].astype(F32).reshape(ROWS, 512) * slope
        row_sum += jnp.sum(grad, axis=1, keepdims=True)
        hi, lo = split(grad)
        gpre[0, x] = hi
        gpre[1, x] = lo
    depth_analyse(2, 1, lambda x, part: gpre[part, x], ((0, 0), (0, 1), (1, 0)))
    start_e(1)
    start_x(2)

    cross = jnp.zeros((ROWS, ROWS), F32)
    for x in range(XC):
        g = (gpre[0, x], gpre[1, x])
        base[x] = dot3(point_t, g)
        cross += dot(g[0], vb[x], NTD) + dot(g[1], vb[x], NTD)
    gather = (
        lax.broadcasted_iota(jnp.int32, (24, ROWS), 1) // YC
        == lax.broadcasted_iota(jnp.int32, (24, ROWS), 0)
    ).astype(F32)
    place = (
        lax.broadcasted_iota(jnp.int32, (ROWS, 128), 0) // YC
        == lax.broadcasted_iota(jnp.int32, (ROWS, 128), 1)
    ).astype(F32)
    lane = lax.broadcasted_iota(jnp.int32, (ROWS, 128), 1)
    both = exact(jnp.where(same_y, cross, 0.0), place) + jnp.where(lane == C, row_sum, 0.0)
    small[0] = exact(gather, both)

    def small_copy(s, k, peer, slot):
        return remote(small.at[s], smalls.at[s, slot], ss_sem.at[s, k], rs_sem.at[s, slot], *peer)

    xpos, zpos = d // ZPOS, lax.rem(d, ZPOS)
    steps = (
        (GY, e, lambda i: (d, i)),
        (XPOS, xpos, lambda i: (i * ZPOS + zpos, e)),
        (ZPOS, zpos, lambda i: (xpos * ZPOS + i, e)),
    )

    def start_small(s):
        count, me, peer_of = steps[s]
        for k in range(1, count):
            small_copy(s, k, peer_of(lax.rem(me + k, count)), me).start()
        smalls[s, me] = small[s]

    def finish_small(s):
        count, me, peer_of = steps[s]
        for k in range(1, count):
            other = lax.rem(me + count - k, count)
            copy = small_copy(s, k, peer_of(other), other)
            copy.wait_recv()
            copy.wait_send()
        total = smalls[s, 0]
        for k in range(1, count):
            total = total + smalls[s, k]
        return total

    start_small(0)
    send_main_then_extra(2, 1)
    small[1] = finish_small(0)
    start_small(1)
    wait_y(1)
    y_analyse(1, grads)

    def mix_back(j):
        real = jnp.zeros((16, 128), F32)
        imag = jnp.zeros((16, 128), F32)
        for o in range(C):
            wr, wi = wp[0, o, j], wp[1, o, j]
            gr, gi = grads[16 * o : 16 * o + 16, 0:128], grads[16 * o : 16 * o + 16, 128:256]
            real += wr * gr + wi * gi
            imag += wr * gi - wi * gr
        at = pl.ds(pl.multiple_of(j * 16, 16), 16)
        mixed[at, 0:128] = jnp.where(valid, real, 0.0)
        mixed[at, 128:256] = jnp.where(valid, imag, 0.0)

    over(C, mix_back)
    y_synthesise(1)
    start_b(1)
    small[2] = finish_small(1)
    start_small(2)
    cells_back(1, 3)

    total = finish_small(2)
    sums[640:664, 0:128] = total
    sums[640:664, 128:256] = jnp.zeros_like(total)

    wait_x(3)
    wait_r(1)
    wait_e_sent(1)
    left = depth_rows(3, 1, XC)
    for x in range(XC):
        total = depth_synthesise(3, 1, x, left) + base[x]
        fields[1, :, x] = total.reshape(C, YC, 512).astype(BF16)


GROUPS = 5


def finish(fields, sums, act, ghist, gs, gpoint, goff, gs_v, io_sem, gs_sem):
    modes, grads = sums.at[0:320], sums.at[320:640]
    copies = [
        pltpu.make_async_copy(fields.at[0], act, io_sem.at[0]),
        pltpu.make_async_copy(fields.at[1], ghist, io_sem.at[1]),
    ]
    for copy in copies:
        copy.start()
    gpoint[...] = sums[640 : 640 + C, 0:C]
    column = sums[640 : 640 + C, C : C + 1]
    diagonal = lax.broadcasted_iota(jnp.int32, (C, C), 0) == lax.broadcasted_iota(
        jnp.int32, (C, C), 1
    )
    goff[...] = jnp.sum(jnp.where(diagonal, column, 0.0), axis=0, keepdims=True)

    def row(o, carry):
        at = pl.ds(pl.multiple_of(o * 16, 16), 16)
        gr = grads[at, 0:128] * (1.0 / CELLS)
        gi = grads[at, 128:256] * (1.0 / CELLS)
        for j in range(C):
            mr, mi = modes[16 * j : 16 * j + 16, 0:128], modes[16 * j : 16 * j + 16, 128:256]
            real = gr * mr + gi * mi
            imag = gi * mr - gr * mi
            for k in range(KX):
                gs_v[0, o, j, k] = real[4 * k : 4 * k + 4, 0:MY]
                gs_v[1, o, j, k] = imag[4 * k : 4 * k + 4, 0:MY]
        return carry

    size = C // GROUPS
    for b in range(GROUPS):
        lax.fori_loop(b * size, (b + 1) * size, row, 0)
        for r in range(2):
            at = pl.ds(b * size, size)
            copy = pltpu.make_async_copy(gs_v.at[r, at], gs.at[r, at], gs_sem.at[r, b])
            copy.start()
            copies.append(copy)
    for copy in copies:
        copy.wait()


def per_device(history, w_point, offset, spectral_weight, cotangent):
    def two(table):
        return jnp.asarray(halves(table))

    xa, xs, xe = x_tables()
    yt = y_table()
    slots = slot_tables()
    weight = jnp.transpose(spectral_weight, (0, 1, 2, 4, 3, 5))
    vmem = pl.BlockSpec(memory_space=pltpu.VMEM)
    hbm = pl.BlockSpec(memory_space=pl.ANY)
    block = jax.ShapeDtypeStruct((C, XC, YC, NZ * NT), BF16)
    square = jax.ShapeDtypeStruct((C, C), F32)
    line = jax.ShapeDtypeStruct((1, C), F32)
    dma = pltpu.SemaphoreType.DMA
    fields, sums = pl.pallas_call(
        kernel,
        out_shape=(jax.ShapeDtypeStruct((2,) + block.shape, BF16), jax.ShapeDtypeStruct((664, 256), F32)),
        in_specs=[vmem] * 4 + [hbm] * 9,
        out_specs=(vmem,) * 2,
        scratch_shapes=[
            pltpu.VMEM((2, 144, 512), BF16),
            pltpu.VMEM((2, 2, 256, 512), BF16),
            pltpu.VMEM((2, 2, 512, 384), BF16),
            pltpu.VMEM((2, 4, 256, 256), BF16),
            pltpu.VMEM((2, 128, 256), BF16),
            pltpu.VMEM((2, 256, 128), BF16),
            pltpu.VMEM((64, 160), BF16),
            pltpu.VMEM((160, 64), BF16),
            pltpu.VMEM((2, C, C, KX, Q, MY), F32),
            pltpu.VMEM((2, C, C, 16, 128), F32),
            pltpu.VMEM((XC, ROWS, 512), BF16),
            pltpu.VMEM((XC, ROWS, 512), F32),
            pltpu.VMEM((2, XC, ROWS, 512), BF16),
            pltpu.VMEM((C * 16, 256), F32),
            pltpu.VMEM((4, GX, XC + 1, 4, 128), F32),
            pltpu.VMEM((4, GX, XC + 1, 4, 128), F32),
            pltpu.VMEM((2, EXTRA, XC + 1, 2, 128), F32),
            pltpu.VMEM((2, GX, XC + 1, 2, 128), F32),
            pltpu.VMEM((2, GX, XC + 1, 2, 128), F32),
            pltpu.VMEM((2, EXTRA, XC + 1, 2, 128), F32),
            pltpu.VMEM((2, GY, 2, 16, 128), F32),
            pltpu.VMEM((2, 4, GY, 16, 128), F32),
            pltpu.VMEM((2, 4, GY, 16, 128), F32),
            pltpu.VMEM((2, 5, GY, 16, 128), F32),
            pltpu.VMEM((2, GY, 2, 16, 128), F32),
            pltpu.VMEM((3, 24, 128), F32),
            pltpu.VMEM((3, 8, 24, 128), F32),
            dma((9,)),
            dma((4, GX)),
            dma((4, GX)),
            dma((2, EXTRA)),
            dma((2, GX)),
            dma((2, GX)),
            dma((2, EXTRA)),
            dma((2, 5, GY)),
            dma((2, 4, GY)),
            dma((2, 4, GY)),
            dma((2, 5, GY)),
            dma((3, 8)),
            dma((3, 8)),
        ],
        compiler_params=pltpu.CompilerParams(
            collective_id=0, has_side_effects=True, vmem_limit_bytes=58 * 1024 * 1024
        ),
    )(
        history[0], cotangent[0], w_point, offset.reshape(1, C), weight,
        two(depth_table()), two(xa), two(xs), two(xe), two(yt), two(yt.T),
        jnp.asarray(slots.astype(ml_dtypes.bfloat16)),
        jnp.asarray(slots.transpose(0, 2, 1).astype(ml_dtypes.bfloat16)),
    )
    act, ghist, gs, gpoint, goff = pl.pallas_call(
        finish,
        out_shape=(
            block, block, jax.ShapeDtypeStruct((2, C, C, KX, Q, MY), F32), square, line,
        ),
        in_specs=[hbm, vmem],
        out_specs=(hbm,) * 3 + (vmem,) * 2,
        scratch_shapes=[pltpu.VMEM((2, C, C, KX, Q, MY), F32), dma((2,)), dma((2, GROUPS))],
        compiler_params=pltpu.CompilerParams(vmem_limit_bytes=16 * 1024 * 1024),
    )(fields, sums)
    grad_spectral = jnp.transpose(gs, (0, 1, 2, 4, 3, 5))
    return act[None], ghist[None], grad_spectral, gpoint, goff.reshape(C)


def solution(mesh):
    grid = P(None, None, "gx", "gy", None)
    modes = P(None, None, None, "gx", "gy", None)
    return jax.shard_map(
        per_device,
        mesh=mesh,
        in_specs=(grid, P(), P(), modes, grid),
        out_specs=(grid, grid, modes, P(), P()),
        check_vma=False,
    )
```

time: 131 us -> 118 us (0.901)
  local copies, waits for them, and re-layouts: 10.6 us -> 2.4 us
  Pallas kernels: 119 us -> 115 us
    unnamed x9 -> x4, local copies, waits for them, and re-layouts: 10.6 us -> 2.4 us
    pallas_call x1 -> x2, Pallas kernels: 119 us -> 115 us  [the longest x1 112 us: per_device(): pl.pallas_call(kernel, out_shape=(jax.ShapeDtypeStruct((2,) + block.shape...]
where the time goes in v2:
time: 118 us
  Pallas kernels  115 us (97%)
  local copies, waits for them, and re-layouts  2.4 us (2%)
    pallas_call x1, Pallas kernels, per_device(): pl.pallas_call(kernel, out_shape=(jax.ShapeDtypeStruct((2,) + block.shape...  112 us
    pallas_call x1, Pallas kernels, per_device(): pl.pallas_call(finish, out_shape=(block, block, jax.ShapeDtypeStruct((2,...  3.33 us
    unnamed x4, local copies, waits for them, and re-layouts  2.4 us

profile of v2, /device:TPU:1, one launch (start us, length us, event | category | flops | bytes accessed | tf_op | source)
XLA Modules:
  0.0 118.1 jit_solution(16802370527850410561)
XLA Ops:
  0.6 111.5 %shard_map.164 = (bf16[2,20,4,8,512]{4,3,2,1,0:T(8,128)(2,1)}, f32[664,256]{1,0:T(8,128)}) custom-call(bf16[20,4,8,512]{3,2,1,0:T(8,128)(2,1)} %bitcast.9, bf16[20,4,8,512]{3,2,1,0:T(8,128)(2,1)} %bitcast.10, f32[20,20]{1,0:T(8,128)} %wpt.1, f32[1,20]{1,0:T(1,128)} %bitcast.11, f32[2,20,20,3,4,24]{5,4,3,2,1,0:T(4,128)} %bitcast.8, ...), custom_call_target="tpu_custom_call" | custom-call | tf_op jit(solution)/shard_map/pallas_call | solution.py:884
  112.2 0.0 copy-start
  112.2 1.3 %copy-done = bf16[2,20,4,8,512]{4,3,2,1,0:T(8,128)(2,1)S(1)} copy-done((bf16[2,20,4,8,512]{4,3,2,1,0:T(8,128)(2,1)S(1)}, bf16[2,20,4,8,512]{4,3,2,1,0:T(8,128)(2,1)}, u32[]{:S(2)}) %copy-start) | copy-done | bytes 1310744
  113.5 0.0 copy-start.1
  113.5 1.1 copy-done.1
  114.6 3.3 %shard_map.165 = (bf16[20,4,8,512]{3,2,1,0:T(8,128)(2,1)}, bf16[20,4,8,512]{3,2,1,0:T(8,128)(2,1)}, f32[2,20,20,3,4,24]{5,4,3,2,1,0:T(4,128)}, f32[20,20]{1,0:T(8,128)}, f32[1,20]{1,0:T(1,128)}) custom-call(bf16[2,20,4,8,512]{4,3,2,1,0:T(8,128)(2,1)S(1)} %copy-done, f32[664,256]{1,0:T(8,128)S(1)} %copy-done.1), custom_call_target="tpu_custom_call" | custom-call | tf_op jit(solution)/shard_map/pallas_call | solution.py:940
Async XLA Ops:
  112.2 1.3 %copy-start = (bf16[2,20,4,8,512]{4,3,2,1,0:T(8,128)(2,1)S(1)}, bf16[2,20,4,8,512]{4,3,2,1,0:T(8,128)(2,1)}, u32[]{:S(2)}) copy-start(bf16[2,20,4,8,512]{4,3,2,1,0:T(8,128)(2,1)} %get-tuple-element.12.fields) | copy-start | bytes 3932164
  113.5 1.1 copy-start.1

commit v3 on v2

--- a/solution.py
+++ b/solution.py
@@ -1,4 +1,4 @@
-import functools
+import math
 
 import jax
 import jax.numpy as jnp
@@ -71,68 +71,54 @@
     x = np.arange(NX).reshape(GX, XC).T
     angle = 2 * np.pi * (fx[:, :, None, None] * x[None, None] % NX) / NX
     cos, sin = np.cos(angle), np.sin(angle)
-    main = np.zeros((GY, 2, 16, XC, GX, 2, 2))
-    extra = np.zeros((2, GY, 2, 16, XC, GX, 2))
+    main = np.zeros((GY, 2, 2, 8, XC, GX, 2, 2))
+    extra = np.zeros((2, GY, 2, 8, XC, GX, 2))
     direct = ((cos, sin), (-sin, cos))
     conj = ((cos, -sin), (-sin, -cos))
     for out in range(2):
         for k in range(KX):
-            row = 6 * out + 2 * k
+            row = KX * out + k
             for into in range(2):
                 for m in range(2):
-                    main[:, 0, row + m, :, :, into, m] = direct[out][into][:, k]
-                    main[:, 1, row + m, :, :, into, m] = conj[out][into][:, k]
+                    main[:, 0, m, row, :, :, into, m] = direct[out][into][:, k]
+                    main[:, 1, m, row, :, :, into, m] = conj[out][into][:, k]
                 extra[1, :, 0, row, :, :, into] = direct[out][into][:, k]
                 extra[1, :, 1, row, :, :, into] = conj[out][into][:, k]
             extra[0, :, 0, row, :, :, 0] = direct[out][0][:, k]
             extra[0, :, 1, row, :, :, 1] = direct[out][0][:, k]
 
-    def spread_rows(full):
-        out = np.zeros((4,) + full.shape[:2] + (4,) + full.shape[3:])
+    def tables(full, columns):
+        blocks = full.size // (GY * 8 * columns)
+        full = full.reshape(GY, blocks, 8, columns)
+        tail = np.zeros((4, GY, blocks, 2, columns))
         for g in range(4):
-            out[g, :, :, :3] = full[:, :, g:12:4]
-        return out
-
-    def both(full):
-        tail = spread_rows(full)
-        columns = full[0, 0, 0].size
-        rows = tail.transpose(0, 2, 1, *range(3, tail.ndim))
-        return (
-            full.reshape(256, columns),
-            tail.reshape(256, columns),
-            full.swapaxes(0, 1).reshape(2, GY * 16, columns),
-            rows.reshape(4, 2, GY * 4, columns),
-        )
-
-    am, al, sm, sl = both(main)
-    sm = np.concatenate([sm[0], sm[1], sm[1]]).T
-    sl = np.concatenate([sl[:, :1], sl[:, 1:], sl[:, 1:]], axis=1).reshape(384, -1).T
-    ex = [both(extra[kind]) for kind in range(2)]
-    em, el = np.stack([v[0] for v in ex]), np.stack([v[1] for v in ex])
-    esm = np.stack([v[2].reshape(256, 256).T for v in ex])
-    esl = np.stack([v[3].reshape(256, 256).T for v in ex])
-    return np.stack([am, al]), np.stack([sm, sl]), np.stack([em, el, esm, esl], axis=1)
-
-
-def slot_tables():
-    maps = (
-        {(0, 0): 0, (0, 1): 3, (1, 0): 1, (1, 1): 2},
-        {(0, 0): 3, (0, 1): 2, (1, 0): 0, (2, 1): 1},
-        {(0, 0): 3, (0, 1): 2, (1, 1): 1, (2, 0): 0},
-        {(0, 0): 0, (0, 1): 1, (1, 0): 2, (1, 1): 3},
-        {(0, 0): 0, (1, 0): 1, (2, 0): 2, (3, 0): 3},
-        {(0, 0): 0, (1, 0): 3, (2, 0): 2, (3, 0): 1},
+            rows = full[:, :, g:6:4]
+            tail[g, :, :, : rows.shape[2]] = rows
+        count = GY * blocks * 8
+        forward = np.stack([full.reshape(count, columns), tail.reshape(count, columns)])
+        backward = np.stack([
+            full.swapaxes(0, 1).reshape(count, columns).T,
+            tail.swapaxes(1, 2).reshape(count, columns).T,
+        ])
+        return forward, backward
+
+    forward, backward = tables(main, XC * GX * 4)
+    extras = [tables(extra[kind], XC * GX * 2) for kind in range(2)]
+    return (
+        forward, backward, np.stack([v[0] for v in extras]), np.stack([v[1] for v in extras])
     )
-    out = np.zeros((len(maps), 64, 160))
-    for kind, table in enumerate(maps):
-        for (slot, m), q in table.items():
-            for ri in range(2):
-                for k in range(KX):
-                    r = 6 * ri + 2 * k + m
-                    at = 16 * ri + 4 * k + q
-                    out[kind, 16 * slot + r, at] = 1
-                    out[kind, 16 * slot + 12 + r // 4, 32 + 32 * (r % 4) + at] = 1
-    return out
+
+
+def slot_table():
+    out = np.zeros((Q, 8, 160))
+    for q in range(Q):
+        for ri in range(2):
+            for k in range(KX):
+                r = KX * ri + k
+                at = 16 * ri + 4 * k + q
+                out[q, r, at] = 1
+                out[q, 6 + r // 4, 32 + 32 * (r % 4) + at] = 1
+    return out.reshape(Q * 8, 160)
 
 
 def y_table():
@@ -189,10 +175,10 @@
 
 
 def kernel(
-    hist, cot, wpt, off, w_hbm, dtab_h, xa_h, xs_h, xe_h, ya_h, ys_h, u_h, ut_h,
+    hist, cot, wpt, off, w_hbm, dtab_h, xa_h, xs_h, xea_h, xes_h, ya_h, ys_h, u_h, ut_h,
     fields, sums,
-    dtab, xa, xs, xe, ya, ys, u, ut, w_v, wp, vb, base, gpre, mixed,
-    sendx, recvx, sende, recve, sendr, recvr, sendy, recvy, backs, backr, exy, small, smalls,
+    dtab, xa, xs, xea, xes, ya, ys, u, ut, w_v, wp, vb, base, gpre, mixed,
+    sendx, recvx, sende, recve, sendr, recvr, sendy, recvy, backs, backr, exy, backx, small, smalls,
     load_sem, sx_sem, rx_sem, se_sem, re_sem, sr_sem, rr_sem, sy_sem, ry_sem, sb_sem, rb_sem, ss_sem, rs_sem,
 ):
     d = lax.axis_index("gx")
@@ -205,7 +191,6 @@
     is_low = d < 2
     special = lax.rem(d, STRIDE) == 0
     which = d // STRIDE
-    kind = jnp.where(is_low, 4 + side, jnp.where(is_mid, 3, jnp.where(is_a, 0, 1 + side)))
     kind_e = jnp.where(d == 0, 0, 1)
     pair = GX - 2 * half
     mirror = GX + 1 - d
@@ -214,19 +199,25 @@
         pltpu.make_async_copy(src, dst, load_sem.at[i])
         for i, (src, dst) in enumerate((
             (dtab_h, dtab), (w_hbm, w_v), (xa_h, xa), (xs_h, xs), (ya_h, ya), (ys_h, ys),
-            (u_h.at[kind], u), (ut_h.at[kind], ut),
+            (u_h, u), (ut_h, ut),
         ))
     ]
-    extra_load = pltpu.make_async_copy(xe_h.at[:, kind_e], xe, load_sem.at[len(loads)])
+    extra_loads = [
+        pltpu.make_async_copy(src.at[:, kind_e], dst, load_sem.at[len(loads) + i])
+        for i, (src, dst) in enumerate(((xea_h, xea), (xes_h, xes)))
+    ]
     for load in loads:
         load.start()
 
     @pl.when(special)
     def _():
-        extra_load.start()
-
-    recvy[...] = jnp.zeros_like(recvy)
-    backr[...] = jnp.zeros_like(backr)
+        for load in extra_loads:
+            load.start()
+
+
+    @pl.when(is_low | is_mid)
+    def _():
+        backr[:, 1] = jnp.zeros_like(backr[:, 1])
 
     barrier = pltpu.get_barrier_semaphore()
 
@@ -321,187 +312,199 @@
         def _():
             over(GX, lambda k: r_copy(f, (d + k) & (GX - 1), which).wait_send(), 1)
 
-    others = jnp.where(is_a, 2, jnp.where(is_mid, 0, 1))
-    own_part = jnp.where(is_b, 1, 0)
-    other_part = jnp.where(is_a, 1, 0)
-    other_slot = jnp.where(is_a, 1 + side, 1)
-
-    def other_at(t):
-        return jnp.where(is_a, pair + t, jnp.where(is_low, d + 16, mirror))
-
-    def y_copy(f, y, part, slot, x, sem):
-        return remote(
-            sendy.at[f, y, part], recvy.at[f, slot, e], sy_sem.at[f, sem, y], ry_sem.at[f, slot, e], x, y
-        )
-
-    def ex_copy(f, y, part):
-        return remote(
-            exy.at[f, y, part], recvy.at[f, which, e], sy_sem.at[f, 3 + part, y],
-            ry_sem.at[f, which, e], part, y,
-        )
+    def owner_of(part, m):
+        if part == 0:
+            x = jnp.where(is_a | is_mid, d, jnp.where(is_low, d + 16, mirror))
+            slot = jnp.where(is_a, 3 * m, jnp.where(is_b, 1 + m, jnp.where(is_mid, m, 2 + m)))
+        else:
+            x = jnp.where(is_a, pair + (side + m) % 2, d)
+            slot = jnp.where(is_a, m, 3 - m)
+        return x, slot
 
     def each_y(f, act_on):
-        def own(k):
+        def block(part, m, y, k):
+            x, slot = owner_of(part, m)
+
+            @pl.when((x != d) | (k != 0))
+            def _():
+                act_on(remote(
+                    sendy.at[f, y, part, m], recvy.at[f, e, slot], sy_sem.at[f, 2 * part + m, y],
+                    ry_sem.at[f, slot, e], x, y,
+                ))
+
+        def go(k):
             y = (e + k) & (GY - 1)
-            act_on(y_copy(f, y, own_part, 0, d, 0))
-
-        @pl.when(d >= 2)
-        def _():
-            over(GY, own, 1)
-
-        def other(k):
-            y = (e + k) & (GY - 1)
-            over(
-                others,
-                lambda t: act_on(y_copy(f, y, other_part, other_slot, other_at(t), 1 + t)),
-            )
-
-        over(GY, other)
+            for m in range(2):
+                block(0, m, y, k)
+
+            @pl.when(is_a | is_b)
+            def _():
+                for m in range(2):
+                    block(1, m, y, k)
+
+        over(GY, go)
 
     def each_ex(f, act_on):
         def go(k):
             y = (e + k) & (GY - 1)
-
-            @pl.when((d != 0) | (k != 0))
-            def _():
-                act_on(ex_copy(f, y, 0))
-
-            act_on(ex_copy(f, y, 1))
+            for part in range(2):
+                slot = which if part == 0 else (4 - which) & 3
+
+                def act_here():
+                    act_on(remote(
+                        exy.at[f, y, part], recvy.at[f, e, slot], sy_sem.at[f, 4 + part, y],
+                        ry_sem.at[f, slot, e], part, y,
+                    ))
+
+                if part == 0:
+                    pl.when((d != 0) | (k != 0))(act_here)
+                else:
+                    act_here()
 
         over(GY, go)
 
     def start_y(f):
         each_y(f, lambda copy: copy.start())
-
-        @pl.when(d >= 2)
-        def _():
-            recvy[f, 0, e] = sendy[f, e, own_part]
+        for part in range(2):
+            for m in range(2):
+                x, slot = owner_of(part, m)
+
+                @pl.when((x == d) & ((part == 0) | is_b))
+                def _():
+                    recvy[f, e, slot] = sendy[f, e, part, m]
 
     def start_ex(f):
         each_ex(f, lambda copy: copy.start())
 
         @pl.when(d == 0)
         def _():
-            recvy[f, 0, e] = exy[f, e, 0]
+            recvy[f, e, 0] = exy[f, e, 0]
 
     def wait_y(f):
-        def arrived(slot, y):
-            remote(
-                sendy.at[f, 0, 0], recvy.at[f, slot, y], sy_sem.at[f, 0, 0], ry_sem.at[f, slot, y], d, y
-            ).wait_recv()
-
-        @pl.when(d >= 1)
-        def _():
-            over(GY, lambda k: arrived(0, (e + GY - k) & (GY - 1)), 1)
-
-        @pl.when(d == 1)
-        def _():
-            arrived(0, e)
-
-        @pl.when(d == 0)
-        def _():
-            over(GY, lambda k: arrived(0, (e + GY - k) & (GY - 1)), 1)
-
-        slots = jnp.where(is_low, 4, jnp.where(is_b, 3, 2))
-
-        def rest(k):
+        def go(k):
             y = (e + GY - k) & (GY - 1)
-            over(slots, lambda slot: arrived(slot, y), 1)
-
-        over(GY, rest)
+            for slot in range(4):
+                own = jnp.where(
+                    is_a, slot in (0, 3), jnp.where(is_b, slot >= 2, jnp.where(is_mid, slot < 2, slot == 0))
+                ) & (d != 1)
+
+                @pl.when((k != 0) | ~own)
+                def _():
+                    remote(
+                        sendy.at[f, 0, 0, 0], recvy.at[f, y, slot], sy_sem.at[f, 0, 0],
+                        ry_sem.at[f, slot, y], d, y,
+                    ).wait_recv()
+
+        over(GY, go)
         each_y(f, lambda copy: copy.wait_send())
 
         @pl.when(special)
         def _():
             each_ex(f, lambda copy: copy.wait_send())
 
-    def b_copy(f, slot, y, x, into):
-        return remote(
-            backs.at[f, slot, y], backr.at[f, into, e], sb_sem.at[f, slot, y], rb_sem.at[f, into, e], x, y
-        )
+    def maker_of(slot):
+        if slot in (1, 2):
+            x = mirror
+            part, m = 0, slot - 1
+        else:
+            x = d
+            part, m = 0, slot // 3
+        if slot < 2:
+            xb, mb = pair + (side + slot) % 2, slot
+        else:
+            xb, mb = d, 3 - slot
+        xm, mm = (d, slot) if slot < 2 else (d - 16, slot - 2)
+        x = jnp.where(is_b, xb, jnp.where(is_mid, xm, x))
+        part = jnp.where(is_b, 1, part)
+        m = jnp.where(is_b, mb, jnp.where(is_mid, mm, m))
+        return x, part, m
 
     def each_b(f, act_on):
-        def own(k):
+        def go(k):
             y = (e + k) & (GY - 1)
-            act_on(b_copy(f, 0, y, d, jnp.where(is_b, 1, 0)))
+
+            @pl.when(d >= 2)
+            def _():
+                for slot in range(4):
+                    x, part, m = maker_of(slot)
+
+                    @pl.when((x != d) | (k != 0))
+                    def _():
+                        act_on(remote(
+                            backs.at[f, y, slot], backr.at[f, part, m, e], sb_sem.at[f, slot, y],
+                            rb_sem.at[f, 2 * part + m, e], x, y,
+                        ))
+
+            @pl.when(is_low)
+            def _():
+                for slot in range(4):
+                    j = jnp.where(d == 0, slot, (4 - slot) & 3)
+
+                    def act_here():
+                        act_on(remote(
+                            backs.at[f, y, slot], backx.at[f, side, e], sb_sem.at[f, slot, y],
+                            rb_sem.at[f, 4 + side, e], j * STRIDE, y,
+                        ))
+
+                    if slot == 0:
+                        pl.when((d != 0) | (k != 0))(act_here)
+                    else:
+                        act_here()
+
+        over(GY, go)
+
+    def start_b(f):
+        each_b(f, lambda copy: copy.start())
 
         @pl.when(d >= 2)
         def _():
-            over(GY, own, 1)
-
-        def other(k):
-            y = (e + k) & (GY - 1)
-
-            @pl.when(is_a | is_mid)
-            def _():
-                act_on(b_copy(f, 1, y, jnp.where(is_a, mirror, d - 16), 0))
-
-            @pl.when(is_b)
-            def _():
-                over(2, lambda t: act_on(b_copy(f, 1 + t, y, pair + t, 1 + side)))
-
-            @pl.when(is_low)
-            def _():
-                def slot(j):
-                    @pl.when((d != 0) | (j != 0) | (k != 0))
-                    def _():
-                        act_on(b_copy(f, j, y, j * STRIDE, 3 + side))
-
-                over(EXTRA, slot)
-
-        over(GY, other)
-
-    def start_b(f):
-        each_b(f, lambda copy: copy.start())
-
-        @pl.when(d >= 2)
-        def _():
-            backr[f, jnp.where(is_b, 1, 0), e] = backs[f, 0, e]
+            for slot in range(4):
+                x, part, m = maker_of(slot)
+
+                @pl.when(x == d)
+                def _():
+                    backr[f, part, m, e] = backs[f, e, slot]
 
         @pl.when(d == 0)
         def _():
-            backr[f, 3, e] = backs[f, 0, e]
+            backx[f, 0, e] = backs[f, e, 0]
 
     def wait_b(f):
-        def arrived(into, y):
-            remote(
-                backs.at[f, 0, 0], backr.at[f, into, y], sb_sem.at[f, 0, 0], rb_sem.at[f, into, y], d, y
-            ).wait_recv()
-
-        def own(k):
-            arrived(jnp.where(is_b, 1, 0), (e + GY - k) & (GY - 1))
-
-        @pl.when(d >= 2)
-        def _():
-            over(GY, own, 1)
-
-        def rest(k):
+        def go(k):
             y = (e + GY - k) & (GY - 1)
 
-            @pl.when(is_a)
-            def _():
-                over(3, lambda into: arrived(into, y), 1)
-
-            @pl.when(is_b | is_low)
-            def _():
-                arrived(0, y)
-
-        over(GY, rest)
+            def arrived(part, m):
+                remote(
+                    backs.at[f, 0, 0], backr.at[f, part, m, y], sb_sem.at[f, 0, 0],
+                    rb_sem.at[f, 2 * part + m, y], d, y,
+                ).wait_recv()
+
+            for m in range(2):
+                @pl.when((k != 0) | is_b | is_low)
+                def _():
+                    arrived(0, m)
+
+                @pl.when(is_a | (is_b & (k != 0)))
+                def _():
+                    arrived(1, m)
+
+        over(GY, go)
         each_b(f, lambda copy: copy.wait_send())
 
     def wait_b_extra(f):
         def go(k):
             y = (e + GY - k) & (GY - 1)
-
-            @pl.when((d != 0) | (k != 0))
-            def _():
-                remote(
-                    backs.at[f, 0, 0], backr.at[f, 3, y], sb_sem.at[f, 0, 0], rb_sem.at[f, 3, y], d, y
-                ).wait_recv()
-
-            remote(
-                backs.at[f, 0, 0], backr.at[f, 4, y], sb_sem.at[f, 0, 0], rb_sem.at[f, 4, y], d, y
-            ).wait_recv()
+            for part in range(2):
+                def arrived():
+                    remote(
+                        backs.at[f, 0, 0], backx.at[f, part, y], sb_sem.at[f, 0, 0],
+                        rb_sem.at[f, 4 + part, y], d, y,
+                    ).wait_recv()
+
+                if part == 0:
+                    pl.when((d != 0) | (k != 0))(arrived)
+                else:
+                    arrived()
 
         over(GY, go)
 
@@ -536,23 +539,25 @@
             ))
             term = dot3((tables[0, 1, :, at], tables[1, 1, :, at]), cols)
             tail = term if tail is None else tail + term
-        out[...] = main.reshape(GY, 2, 16, 128)
+        blocks = out.shape[:-2]
+        size = tail.shape[0] // 4
+        out[...] = main.reshape(blocks + (8, 128))
         tail = jnp.where(lane128 < 32, tail, 0.0)
-        packed = tail[0:64]
+        packed = tail[0:size]
         for g in range(1, 4):
-            packed = packed + pltpu.roll(tail[64 * g : 64 * g + 64], 32 * g, 1)
-        out[:, :, 12:16, :] = packed.reshape(GY, 2, 4, 128)
+            packed = packed + pltpu.roll(tail[size * g : size * g + size], 32 * g, 1)
+        out[..., 6:8, :] = packed.reshape(blocks + (2, 128))
 
     def analyse_main(p, f):
         x_analyse([recvx[p, :, t].reshape(128, 128) for t in range(XC + 1)], xa, sendy.at[f])
 
     def analyse_extra(f):
         x_analyse(
-            [recve[f, :, t].reshape(64, 128) for t in range(XC + 1)], xe.at[:, 0:2], exy.at[f]
+            [recve[f, :, t].reshape(64, 128) for t in range(XC + 1)], xea, exy.at[f]
         )
 
     def y_analyse(f, out):
-        cols = split(jnp.concatenate([recvy[f, :, y].reshape(64, 128) for y in range(GY)], axis=1))
+        cols = split(jnp.concatenate([recvy[f, y].reshape(32, 128) for y in range(GY)], axis=1))
         merged = dot2(ut[...], cols)
         rows = []
         parts = [
@@ -587,13 +592,13 @@
             stack.append(jnp.concatenate(rows, axis=0))
         out = dot2(u[...], split(jnp.concatenate(stack, axis=1)))
         for y in range(GY):
-            backs[f, :, y] = out[:, 128 * y : 128 * y + 128].reshape(4, 16, 128)
+            backs[f, y] = out[:, 128 * y : 128 * y + 128].reshape(4, 8, 128)
 
     def x_synthesise(slots, tables, put):
-        count = slots.shape[0] * GY
         rows = slots[...]
-        main_cols = split(rows.reshape(count * 16, 128))
-        tail = rows[:, :, 12:16, :].reshape(count * 4, 128)
+        count = math.prod(rows.shape[:-2])
+        main_cols = split(rows.reshape(count * 8, 128))
+        tail = rows[..., 6:8, :].reshape(count * 2, 128)
         tail_cols = split(jnp.concatenate(
             [tail] + [pltpu.roll(tail, 128 - 32 * g, 1) for g in range(1, 4)], axis=0
         ))
@@ -613,13 +618,13 @@
         def put(t, rows):
             sendx[p, :, t] = rows.reshape(GX, 4, 128)
 
-        x_synthesise(backr.at[f, 0:3], xs, put)
+        x_synthesise(backr.at[f], xs, put)
 
     def synthesise_extra(f):
         def put(t, rows):
             sendr[f, :, t] = rows.reshape(GX, 2, 128)
 
-        x_synthesise(backr.at[f, 3:5], xe.at[:, 2:4], put)
+        x_synthesise(backx.at[f], xes, put)
 
     def depth_rows(p, f, t):
         tile = recvx[p, :, t].reshape(128, 128)
@@ -668,7 +673,8 @@
 
     @pl.when(special)
     def _():
-        extra_load.wait()
+        for load in extra_loads:
+            load.wait()
 
     def pack(o):
         for r in range(2):
@@ -871,9 +877,9 @@
     def two(table):
         return jnp.asarray(halves(table))
 
-    xa, xs, xe = x_tables()
+    xa, xs, xea, xes = x_tables()
     yt = y_table()
-    slots = slot_tables()
+    slots = slot_table()
     weight = jnp.transpose(spectral_weight, (0, 1, 2, 4, 3, 5))
     vmem = pl.BlockSpec(memory_space=pltpu.VMEM)
     hbm = pl.BlockSpec(memory_space=pl.ANY)
@@ -884,17 +890,18 @@
     fields, sums = pl.pallas_call(
         kernel,
         out_shape=(jax.ShapeDtypeStruct((2,) + block.shape, BF16), jax.ShapeDtypeStruct((664, 256), F32)),
-        in_specs=[vmem] * 4 + [hbm] * 9,
+        in_specs=[vmem] * 4 + [hbm] * 10,
         out_specs=(vmem,) * 2,
         scratch_shapes=[
             pltpu.VMEM((2, 144, 512), BF16),
             pltpu.VMEM((2, 2, 256, 512), BF16),
-            pltpu.VMEM((2, 2, 512, 384), BF16),
-            pltpu.VMEM((2, 4, 256, 256), BF16),
+            pltpu.VMEM((2, 2, 512, 256), BF16),
+            pltpu.VMEM((2, 2, 128, 256), BF16),
+            pltpu.VMEM((2, 2, 256, 128), BF16),
             pltpu.VMEM((2, 128, 256), BF16),
             pltpu.VMEM((2, 256, 128), BF16),
-            pltpu.VMEM((64, 160), BF16),
-            pltpu.VMEM((160, 64), BF16),
+            pltpu.VMEM((32, 160), BF16),
+            pltpu.VMEM((160, 32), BF16),
             pltpu.VMEM((2, C, C, KX, Q, MY), F32),
             pltpu.VMEM((2, C, C, 16, 128), F32),
             pltpu.VMEM((XC, ROWS, 512), BF16),
@@ -907,24 +914,25 @@
             pltpu.VMEM((2, GX, XC + 1, 2, 128), F32),
             pltpu.VMEM((2, GX, XC + 1, 2, 128), F32),
             pltpu.VMEM((2, EXTRA, XC + 1, 2, 128), F32),
-            pltpu.VMEM((2, GY, 2, 16, 128), F32),
-            pltpu.VMEM((2, 4, GY, 16, 128), F32),
-            pltpu.VMEM((2, 4, GY, 16, 128), F32),
-            pltpu.VMEM((2, 5, GY, 16, 128), F32),
-            pltpu.VMEM((2, GY, 2, 16, 128), F32),
+            pltpu.VMEM((2, GY, 2, 2, 8, 128), F32),
+            pltpu.VMEM((2, GY, Q, 8, 128), F32),
+            pltpu.VMEM((2, GY, Q, 8, 128), F32),
+            pltpu.VMEM((2, 2, 2, GY, 8, 128), F32),
+            pltpu.VMEM((2, GY, 2, 8, 128), F32),
+            pltpu.VMEM((2, 2, GY, 8, 128), F32),
             pltpu.VMEM((3, 24, 128), F32),
             pltpu.VMEM((3, 8, 24, 128), F32),
-            dma((9,)),
+            dma((10,)),
             dma((4, GX)),
             dma((4, GX)),
             dma((2, EXTRA)),
             dma((2, GX)),
             dma((2, GX)),
             dma((2, EXTRA)),
-            dma((2, 5, GY)),
+            dma((2, 6, GY)),
             dma((2, 4, GY)),
             dma((2, 4, GY)),
-            dma((2, 5, GY)),
+            dma((2, 6, GY)),
             dma((3, 8)),
             dma((3, 8)),
         ],
@@ -933,9 +941,9 @@
         ),
     )(
         history[0], cotangent[0], w_point, offset.reshape(1, C), weight,
-        two(depth_table()), two(xa), two(xs), two(xe), two(yt), two(yt.T),
+        two(depth_table()), two(xa), two(xs), two(xea), two(xes), two(yt), two(yt.T),
         jnp.asarray(slots.astype(ml_dtypes.bfloat16)),
-        jnp.asarray(slots.transpose(0, 2, 1).astype(ml_dtypes.bfloat16)),
+        jnp.asarray(slots.T.astype(ml_dtypes.bfloat16)),
     )
     act, ghist, gs, gpoint, goff = pl.pallas_call(
         finish,

time: 118 us -> 112 us (0.949)
  Pallas kernels: 115 us -> 108 us
    pallas_call x1, Pallas kernels: 112 us -> 105 us  [per_device(): pl.pallas_call(kernel, out_shape=(jax.ShapeDtypeStruct((2,) + block.shape...]
where the time goes in v3:
time: 112 us; the launch traced here: 111 us
  Pallas kernels  108 us (96%)
  local copies, waits for them, and re-layouts  2.4 us (2%)
    pallas_call x1, Pallas kernels, per_device(): pl.pallas_call(kernel, out_shape=(jax.ShapeDtypeStruct((2,) + block.shape...  105 us
    pallas_call x1, Pallas kernels, per_device(): pl.pallas_call(finish, out_shape=(block, block, jax.ShapeDtypeStruct((2,...  3.33 us
    unnamed x4, local copies, waits for them, and re-layouts  2.4 us

profile of v3, /device:TPU:1, one launch (start us, length us, event | category | flops | bytes accessed | tf_op | source)
XLA Modules:
  0.0 111.5 jit_solution(14863041706929195753)
XLA Ops:
  0.6 104.9 %shard_map.173 = (bf16[2,20,4,8,512]{4,3,2,1,0:T(8,128)(2,1)}, f32[664,256]{1,0:T(8,128)}) custom-call(bf16[20,4,8,512]{3,2,1,0:T(8,128)(2,1)} %bitcast.9, bf16[20,4,8,512]{3,2,1,0:T(8,128)(2,1)} %bitcast.10, f32[20,20]{1,0:T(8,128)} %wpt.1, f32[1,20]{1,0:T(1,128)} %bitcast.11, f32[2,20,20,3,4,24]{5,4,3,2,1,0:T(4,128)} %bitcast.8, ...), custom_call_target="tpu_custom_call" | custom-call | tf_op jit(solution)/shard_map/pallas_call | solution.py:890
  105.6 0.0 copy-start
  105.6 1.3 %copy-done = bf16[2,20,4,8,512]{4,3,2,1,0:T(8,128)(2,1)S(1)} copy-done((bf16[2,20,4,8,512]{4,3,2,1,0:T(8,128)(2,1)S(1)}, bf16[2,20,4,8,512]{4,3,2,1,0:T(8,128)(2,1)}, u32[]{:S(2)}) %copy-start) | copy-done | bytes 1310744
  106.9 0.0 copy-start.1
  106.9 1.1 copy-done.1
  108.0 3.3 %shard_map.174 = (bf16[20,4,8,512]{3,2,1,0:T(8,128)(2,1)}, bf16[20,4,8,512]{3,2,1,0:T(8,128)(2,1)}, f32[2,20,20,3,4,24]{5,4,3,2,1,0:T(4,128)}, f32[20,20]{1,0:T(8,128)}, f32[1,20]{1,0:T(1,128)}) custom-call(bf16[2,20,4,8,512]{4,3,2,1,0:T(8,128)(2,1)S(1)} %copy-done, f32[664,256]{1,0:T(8,128)S(1)} %copy-done.1), custom_call_target="tpu_custom_call" | custom-call | tf_op jit(solution)/shard_map/pallas_call | solution.py:948
Async XLA Ops:
  105.6 1.3 %copy-start = (bf16[2,20,4,8,512]{4,3,2,1,0:T(8,128)(2,1)S(1)}, bf16[2,20,4,8,512]{4,3,2,1,0:T(8,128)(2,1)}, u32[]{:S(2)}) copy-start(bf16[2,20,4,8,512]{4,3,2,1,0:T(8,128)(2,1)} %get-tuple-element.12.fields) | copy-start | bytes 3932164
  106.9 1.1 copy-start.1

commit v4 on v3

--- a/solution.py
+++ b/solution.py
@@ -121,16 +121,17 @@
     return out.reshape(Q * 8, 160)
 
 
-def y_table():
+def y_tables():
     fy = kept(NY, MY)
     angle = 2 * np.pi * (np.arange(NY)[:, None] * fy[None] % NY) / NY
     cos, sin = np.cos(angle), np.sin(angle)
-    out = np.zeros((2, NY, 2, 128))
-    out[0, :, 0, :MY] = cos
-    out[1, :, 0, :MY] = sin
-    out[0, :, 1, :MY] = -sin
-    out[1, :, 1, :MY] = cos
-    return out.reshape(2 * NY, 256)
+    out = np.zeros((4, 2, NY, 2, 4, 32))
+    for g in range(4):
+        out[g, 0, :, 0, g, :MY] = cos
+        out[g, 1, :, 0, g, :MY] = sin
+        out[g, 0, :, 1, g, :MY] = -sin
+        out[g, 1, :, 1, g, :MY] = cos
+    return out.reshape(8 * NY, 256), out.sum(axis=0).reshape(2 * NY, 256)
 
 
 def split(value):
@@ -165,6 +166,11 @@
             if i & s:
                 continue
             a, b = parts[i], parts[i + s]
+            if b is None:
+                if a is not None:
+                    parts[i] = jnp.where(low, a, 0.0)
+                    parts[i + s] = jnp.where(low, pltpu.roll(a, 128 - 8 * s, 1), 0.0)
+                continue
             parts[i] = jnp.where(low, a, pltpu.roll(b, 8 * s, 1))
             parts[i + s] = jnp.where(low, pltpu.roll(a, 128 - 8 * s, 1), b)
     return parts
@@ -175,15 +181,15 @@
 
 
 def kernel(
-    hist, cot, wpt, off, w_hbm, dtab_h, xa_h, xs_h, xea_h, xes_h, ya_h, ys_h, u_h, ut_h,
+    hist, cot, wpt, off, w_hbm, dtab_h, xa_h, xs_h, xea_h, xes_h, ya_h, yar_h, ys_h, ysr_h, u_h, ut_h,
     fields, sums,
-    dtab, xa, xs, xea, xes, ya, ys, u, ut, w_v, wp, vb, base, gpre, mixed,
+    dtab, xa, xs, xea, xes, ya, yar, ys, ysr, u, ut, w_v, wp, vb, base, gpre, mixed,
     sendx, recvx, sende, recve, sendr, recvr, sendy, recvy, backs, backr, exy, backx, small, smalls,
     load_sem, sx_sem, rx_sem, se_sem, re_sem, sr_sem, rr_sem, sy_sem, ry_sem, sb_sem, rb_sem, ss_sem, rs_sem,
 ):
     d = lax.axis_index("gx")
     e = lax.axis_index("gy")
-    modes, grads = sums.at[0:320], sums.at[320:640]
+    modes, grads = sums.at[0:80], sums.at[80:400]
     half, side = d // 2, lax.rem(d, 2)
     is_a = (d >= 2) & (d < 16)
     is_b = d >= 18
@@ -198,7 +204,7 @@
     loads = [
         pltpu.make_async_copy(src, dst, load_sem.at[i])
         for i, (src, dst) in enumerate((
-            (dtab_h, dtab), (w_hbm, w_v), (xa_h, xa), (xs_h, xs), (ya_h, ya), (ys_h, ys),
+            (dtab_h, dtab), (w_hbm, w_v), (xa_h, xa), (xs_h, xs), (ya_h, ya), (yar_h, yar), (ys_h, ys), (ysr_h, ysr),
             (u_h, u), (ut_h, ut),
         ))
     ]
@@ -556,7 +562,7 @@
             [recve[f, :, t].reshape(64, 128) for t in range(XC + 1)], xea, exy.at[f]
         )
 
-    def y_analyse(f, out):
+    def y_cells(f):
         cols = split(jnp.concatenate([recvy[f, y].reshape(32, 128) for y in range(GY)], axis=1))
         merged = dot2(ut[...], cols)
         rows = []
@@ -574,15 +580,11 @@
                 total = total + pltpu.roll(merged[at + 32 * n : at + 32 * n + 16, lanes], 128 - 32 * n, 1)
             parts.append(total)
         rows += swap_groups([jnp.where(lane128 < 32, part, 0.0) for part in parts])[: C - 16]
-        out[...] = dot3(split(jnp.concatenate(rows, axis=0)), (ya[0], ya[1]))
-
-    def y_synthesise(f):
-        cols = dot3(split(mixed[...]), (ys[0], ys[1]))
-        blank = jnp.zeros((16, 128), F32)
-        main = swap_groups([cols[16 * c : 16 * c + 16] for c in range(16)])
-        tail = swap_groups(
-            [cols[16 * c : 16 * c + 16] for c in range(16, C)] + [blank] * (32 - C)
-        )
+        return rows
+
+    def y_synthesise(f, cols):
+        main = swap_groups(cols[:16])
+        tail = swap_groups(cols[16:] + [None] * (32 - C))
         stack = []
         for y in range(GY):
             rows = [main[y], main[GY + y]]
@@ -676,11 +678,14 @@
         for load in extra_loads:
             load.wait()
 
+    wp[...] = jnp.zeros_like(wp)
+
     def pack(o):
         for r in range(2):
             for i in range(C):
+                lanes = slice(32 * (i % 4), 32 * (i % 4) + MY)
                 for k in range(KX):
-                    wp[r, o, i, 4 * k : 4 * k + 4, 0:MY] = w_v[r, o, i, k]
+                    wp[r, o, i // 4, 4 * k : 4 * k + 4, lanes] = w_v[r, o, i, k]
 
     over(C, pack)
 
@@ -701,26 +706,27 @@
 
     send_main_then_extra(0, 0)
     wait_y(0)
-    y_analyse(0, modes)
-
-    valid = (lax.broadcasted_iota(jnp.int32, (16, 128), 0) < 4 * KX) & (
-        lax.broadcasted_iota(jnp.int32, (16, 128), 1) < MY
+    cells = y_cells(0)
+    cells = jnp.concatenate(
+        [jnp.concatenate(cells[i : i + 4], axis=1) for i in range(0, C, 4)], axis=0
     )
+    modes[...] = dot3(split(cells), (ya[0], ya[1]))
 
     def mix(o):
         real = jnp.zeros((16, 128), F32)
         imag = jnp.zeros((16, 128), F32)
-        for i in range(C):
+        for i in range(C // 4):
             wr, wi = wp[0, o, i], wp[1, o, i]
             mr, mi = modes[16 * i : 16 * i + 16, 0:128], modes[16 * i : 16 * i + 16, 128:256]
             real += wr * mr - wi * mi
             imag += wr * mi + wi * mr
         at = pl.ds(pl.multiple_of(o * 16, 16), 16)
-        mixed[at, 0:128] = jnp.where(valid, real, 0.0)
-        mixed[at, 128:256] = jnp.where(valid, imag, 0.0)
+        mixed[at, 0:128] = real
+        mixed[at, 128:256] = imag
 
     over(C, mix)
-    y_synthesise(0)
+    cols = dot3(split(mixed[...]), (ysr[0], ysr[1]))
+    y_synthesise(0, [cols[16 * c : 16 * c + 16] for c in range(C)])
     start_b(0)
     cells_back(0, 1)
     wait_x(1)
@@ -796,7 +802,7 @@
     small[1] = finish_small(0)
     start_small(1)
     wait_y(1)
-    y_analyse(1, grads)
+    grads[...] = dot3(split(jnp.concatenate(y_cells(1), axis=0)), (yar[0], yar[1]))
 
     def mix_back(j):
         real = jnp.zeros((16, 128), F32)
@@ -807,19 +813,22 @@
             real += wr * gr + wi * gi
             imag += wr * gi - wi * gr
         at = pl.ds(pl.multiple_of(j * 16, 16), 16)
-        mixed[at, 0:128] = jnp.where(valid, real, 0.0)
-        mixed[at, 128:256] = jnp.where(valid, imag, 0.0)
-
-    over(C, mix_back)
-    y_synthesise(1)
+        mixed[at, 0:128] = real
+        mixed[at, 128:256] = imag
+
+    over(C // 4, mix_back)
+    cols = dot3(split(mixed[0:80]), (ys[0], ys[1]))
+    y_synthesise(1, [
+        cols[16 * (c // 4) : 16 * (c // 4) + 16, 128 * (c % 4) : 128 * (c % 4) + 128] for c in range(C)
+    ])
     start_b(1)
     small[2] = finish_small(1)
     start_small(2)
     cells_back(1, 3)
 
     total = finish_small(2)
-    sums[640:664, 0:128] = total
-    sums[640:664, 128:256] = jnp.zeros_like(total)
+    sums[400:424, 0:128] = total
+    sums[400:424, 128:256] = jnp.zeros_like(total)
 
     wait_x(3)
     wait_r(1)
@@ -833,20 +842,26 @@
 GROUPS = 5
 
 
-def finish(fields, sums, act, ghist, gs, gpoint, goff, gs_v, io_sem, gs_sem):
-    modes, grads = sums.at[0:320], sums.at[320:640]
+def finish(fields, sums, act, ghist, gs, gpoint, goff, modes, gs_v, io_sem, gs_sem):
+    grads = sums.at[80:400]
     copies = [
         pltpu.make_async_copy(fields.at[0], act, io_sem.at[0]),
         pltpu.make_async_copy(fields.at[1], ghist, io_sem.at[1]),
     ]
     for copy in copies:
         copy.start()
-    gpoint[...] = sums[640 : 640 + C, 0:C]
-    column = sums[640 : 640 + C, C : C + 1]
+    gpoint[...] = sums[400 : 400 + C, 0:C]
+    column = sums[400 : 400 + C, C : C + 1]
     diagonal = lax.broadcasted_iota(jnp.int32, (C, C), 0) == lax.broadcasted_iota(
         jnp.int32, (C, C), 1
     )
     goff[...] = jnp.sum(jnp.where(diagonal, column, 0.0), axis=0, keepdims=True)
+
+    for j in range(C):
+        for half in range(2):
+            lanes = slice(128 * half, 128 * half + 128)
+            tile = sums[16 * (j // 4) : 16 * (j // 4) + 16, lanes]
+            modes[16 * j : 16 * j + 16, lanes] = tile if j % 4 == 0 else pltpu.roll(tile, 128 - 32 * (j % 4), 1)
 
     def row(o, carry):
         at = pl.ds(pl.multiple_of(o * 16, 16), 16)
@@ -878,7 +893,7 @@
         return jnp.asarray(halves(table))
 
     xa, xs, xea, xes = x_tables()
-    yt = y_table()
+    ya, yar = y_tables()
     slots = slot_table()
     weight = jnp.transpose(spectral_weight, (0, 1, 2, 4, 3, 5))
     vmem = pl.BlockSpec(memory_space=pltpu.VMEM)
@@ -889,8 +904,8 @@
     dma = pltpu.SemaphoreType.DMA
     fields, sums = pl.pallas_call(
         kernel,
-        out_shape=(jax.ShapeDtypeStruct((2,) + block.shape, BF16), jax.ShapeDtypeStruct((664, 256), F32)),
-        in_specs=[vmem] * 4 + [hbm] * 10,
+        out_shape=(jax.ShapeDtypeStruct((2,) + block.shape, BF16), jax.ShapeDtypeStruct((424, 256), F32)),
+        in_specs=[vmem] * 4 + [hbm] * 12,
         out_specs=(vmem,) * 2,
         scratch_shapes=[
             pltpu.VMEM((2, 144, 512), BF16),
@@ -898,12 +913,14 @@
             pltpu.VMEM((2, 2, 512, 256), BF16),
             pltpu.VMEM((2, 2, 128, 256), BF16),
             pltpu.VMEM((2, 2, 256, 128), BF16),
+            pltpu.VMEM((2, 512, 256), BF16),
             pltpu.VMEM((2, 128, 256), BF16),
+            pltpu.VMEM((2, 256, 512), BF16),
             pltpu.VMEM((2, 256, 128), BF16),
             pltpu.VMEM((32, 160), BF16),
             pltpu.VMEM((160, 32), BF16),
             pltpu.VMEM((2, C, C, KX, Q, MY), F32),
-            pltpu.VMEM((2, C, C, 16, 128), F32),
+            pltpu.VMEM((2, C, C // 4, 16, 128), F32),
             pltpu.VMEM((XC, ROWS, 512), BF16),
             pltpu.VMEM((XC, ROWS, 512), F32),
             pltpu.VMEM((2, XC, ROWS, 512), BF16),
@@ -922,7 +939,7 @@
             pltpu.VMEM((2, 2, GY, 8, 128), F32),
             pltpu.VMEM((3, 24, 128), F32),
             pltpu.VMEM((3, 8, 24, 128), F32),
-            dma((10,)),
+            dma((12,)),
             dma((4, GX)),
             dma((4, GX)),
             dma((2, EXTRA)),
@@ -941,7 +958,7 @@
         ),
     )(
         history[0], cotangent[0], w_point, offset.reshape(1, C), weight,
-        two(depth_table()), two(xa), two(xs), two(xea), two(xes), two(yt), two(yt.T),
+        two(depth_table()), two(xa), two(xs), two(xea), two(xes), two(ya), two(yar), two(ya.T), two(yar.T),
         jnp.asarray(slots.astype(ml_dtypes.bfloat16)),
         jnp.asarray(slots.T.astype(ml_dtypes.bfloat16)),
     )
@@ -950,10 +967,12 @@
         out_shape=(
             block, block, jax.ShapeDtypeStruct((2, C, C, KX, Q, MY), F32), square, line,
         ),
-        in_specs=[hbm, vmem],
+        in_specs=[vmem, vmem],
         out_specs=(hbm,) * 3 + (vmem,) * 2,
-        scratch_shapes=[pltpu.VMEM((2, C, C, KX, Q, MY), F32), dma((2,)), dma((2, GROUPS))],
-        compiler_params=pltpu.CompilerParams(vmem_limit_bytes=16 * 1024 * 1024),
+        scratch_shapes=[
+            pltpu.VMEM((C * 16, 256), F32), pltpu.VMEM((2, C, C, KX, Q, MY), F32), dma((2,)), dma((2, GROUPS)),
+        ],
+        compiler_params=pltpu.CompilerParams(vmem_limit_bytes=60 * 1024 * 1024),
     )(fields, sums)
     grad_spectral = jnp.transpose(gs, (0, 1, 2, 4, 3, 5))
     return act[None], ghist[None], grad_spectral, gpoint, goff.reshape(C)

time: 112 us -> 108 us (0.964)
  local copies, waits for them, and re-layouts: 2.4 us -> 0 us
    pallas_call x1, Pallas kernels: 105 us -> 102 us  [per_device(): pl.pallas_call(kernel, out_shape=(jax.ShapeDtypeStruct((2,) + block.shape...]
    unnamed x4 -> x0, local copies, waits for them, and re-layouts: 2.4 us -> none
    pallas_call x1, Pallas kernels: 3.33 us -> 4.73 us  [per_device(): pl.pallas_call(finish, out_shape=(block, block, jax.ShapeDtypeStruct((2,...]
where the time goes in v4:
time: 108 us
  Pallas kernels  107 us (99%)
    pallas_call x1, Pallas kernels, per_device(): pl.pallas_call(kernel, out_shape=(jax.ShapeDtypeStruct((2,) + block.shape...  102 us
    pallas_call x1, Pallas kernels, per_device(): pl.pallas_call(finish, out_shape=(block, block, jax.ShapeDtypeStruct((2,...  4.73 us

profile of v4, /device:TPU:1, one launch (start us, length us, event | category | flops | bytes accessed | tf_op | source)
XLA Modules:
  0.0 107.6 jit_solution(8212132453795966654)
XLA Ops:
  0.6 102.1 %shard_map.191 = (bf16[2,20,4,8,512]{4,3,2,1,0:T(8,128)(2,1)}, f32[424,256]{1,0:T(8,128)}) custom-call(bf16[20,4,8,512]{3,2,1,0:T(8,128)(2,1)} %bitcast.9, bf16[20,4,8,512]{3,2,1,0:T(8,128)(2,1)} %bitcast.10, f32[20,20]{1,0:T(8,128)} %wpt.1, f32[1,20]{1,0:T(1,128)} %bitcast.11, f32[2,20,20,3,4,24]{5,4,3,2,1,0:T(4,128)} %bitcast.8, ...), custom_call_target="tpu_custom_call" | custom-call | tf_op jit(solution)/shard_map/pallas_call | solution.py:905
  102.7 4.7 %shard_map.192 = (bf16[20,4,8,512]{3,2,1,0:T(8,128)(2,1)}, bf16[20,4,8,512]{3,2,1,0:T(8,128)(2,1)}, f32[2,20,20,3,4,24]{5,4,3,2,1,0:T(4,128)}, f32[20,20]{1,0:T(8,128)}, f32[1,20]{1,0:T(1,128)}) custom-call(bf16[2,20,4,8,512]{4,3,2,1,0:T(8,128)(2,1)} %get-tuple-element.12.fields, f32[424,256]{1,0:T(8,128)} %get-tuple-element.13.sums), custom_call_target="tpu_custom_call" | custom-call | tf_op jit(solution)/shard_map/pallas_call | solution.py:965

commit v5 on v4

--- a/solution.py
+++ b/solution.py
@@ -181,9 +181,9 @@
 
 
 def kernel(
-    hist, cot, wpt, off, w_hbm, dtab_h, xa_h, xs_h, xea_h, xes_h, ya_h, yar_h, ys_h, ysr_h, u_h, ut_h,
+    hist_h, cot_h, wpt, off, w_hbm, dtab_h, xa_h, xs_h, xea_h, xes_h, ya_h, yar_h, ys_h, ysr_h, u_h, ut_h,
     fields, sums,
-    dtab, xa, xs, xea, xes, ya, yar, ys, ysr, u, ut, w_v, wp, vb, base, gpre, mixed,
+    hist, cot, dtab, xa, xs, xea, xes, ya, yar, ys, ysr, u, ut, w_v, wp, vb, base, gpre, mixed,
     sendx, recvx, sende, recve, sendr, recvr, sendy, recvy, backs, backr, exy, backx, small, smalls,
     load_sem, sx_sem, rx_sem, se_sem, re_sem, sr_sem, rr_sem, sy_sem, ry_sem, sb_sem, rb_sem, ss_sem, rs_sem,
 ):
@@ -201,10 +201,25 @@
     pair = GX - 2 * half
     mirror = GX + 1 - d
 
+    barrier = pltpu.get_barrier_semaphore()
+
+    def signal(x, y):
+        pl.semaphore_signal(barrier, inc=1, device_id=(x, y), device_id_type=MESH)
+
+    def over(count, body, first=0):
+        def go(k, carry):
+            body(k)
+            return carry
+
+        lax.fori_loop(first, count, go, 0)
+
+    over(GX, lambda k: signal((d + k) & (GX - 1), e), 1)
+    over(GY, lambda k: signal(d, (e + k) & (GY - 1)), 1)
+
     loads = [
         pltpu.make_async_copy(src, dst, load_sem.at[i])
         for i, (src, dst) in enumerate((
-            (dtab_h, dtab), (w_hbm, w_v), (xa_h, xa), (xs_h, xs), (ya_h, ya), (yar_h, yar), (ys_h, ys), (ysr_h, ysr),
+            (hist_h, hist), (dtab_h, dtab), (cot_h, cot), (w_hbm, w_v), (xa_h, xa), (xs_h, xs), (ya_h, ya), (yar_h, yar), (ys_h, ys), (ysr_h, ysr),
             (u_h, u), (ut_h, ut),
         ))
     ]
@@ -225,20 +240,6 @@
     def _():
         backr[:, 1] = jnp.zeros_like(backr[:, 1])
 
-    barrier = pltpu.get_barrier_semaphore()
-
-    def signal(x, y):
-        pl.semaphore_signal(barrier, inc=1, device_id=(x, y), device_id_type=MESH)
-
-    def over(count, body, first=0):
-        def go(k, carry):
-            body(k)
-            return carry
-
-        lax.fori_loop(first, count, go, 0)
-
-    over(GX, lambda k: signal((d + k) & (GX - 1), e), 1)
-    over(GY, lambda k: signal(d, (e + k) & (GY - 1)), 1)
     def remote(src, dst, send, recv, x, y):
         return pltpu.make_async_remote_copy(
             src_ref=src, dst_ref=dst, send_sem=send, recv_sem=recv,
@@ -257,11 +258,12 @@
     def wait_x(p):
         def go(k):
             peer = (d + GX - k) & (GX - 1)
-            copy = x_copy(p, peer, peer)
-            copy.wait_recv()
-            copy.wait_send()
+            x_copy(p, peer, peer).wait_recv()
 
         over(GX, go, 1)
+
+    def wait_x_sent(p):
+        over(GX, lambda k: x_copy(p, (d + k) & (GX - 1), d).wait_send(), 1)
 
     def e_copy(f, j, slot):
         return remote(
@@ -402,11 +404,6 @@
                     ).wait_recv()
 
         over(GY, go)
-        each_y(f, lambda copy: copy.wait_send())
-
-        @pl.when(special)
-        def _():
-            each_ex(f, lambda copy: copy.wait_send())
 
     def maker_of(slot):
         if slot in (1, 2):
@@ -495,7 +492,14 @@
                     arrived(1, m)
 
         over(GY, go)
+
+    def wait_sent(f):
+        each_y(f, lambda copy: copy.wait_send())
         each_b(f, lambda copy: copy.wait_send())
+
+        @pl.when(special)
+        def _():
+            each_ex(f, lambda copy: copy.wait_send())
 
     def wait_b_extra(f):
         def go(k):
@@ -661,16 +665,17 @@
         synthesise_main(f, p)
         start_x(p)
 
+    loads[0].wait()
     for x in range(XC):
         vb[x] = hist[:, x].astype(F32).reshape(ROWS, 512).astype(BF16)
-    loads[0].wait()
+    loads[1].wait()
     depth_analyse(0, 0, lambda x, part: vb[x], ((0, 0), (1, 0)))
 
     pl.semaphore_wait(barrier, GX + GY - 2)
     start_e(0)
     start_x(0)
 
-    for load in loads[1:]:
+    for load in loads[2:]:
         load.wait()
 
     @pl.when(special)
@@ -731,7 +736,6 @@
     cells_back(0, 1)
     wait_x(1)
     wait_r(0)
-    wait_e_sent(0)
 
     left = depth_rows(1, 0, XC)
     row_sum = jnp.zeros((ROWS, 1), F32)
@@ -751,6 +755,9 @@
     depth_analyse(2, 1, lambda x, part: gpre[part, x], ((0, 0), (0, 1), (1, 0)))
     start_e(1)
     start_x(2)
+    wait_sent(0)
+    wait_x_sent(0)
+    wait_x_sent(1)
 
     cross = jnp.zeros((ROWS, ROWS), F32)
     for x in range(XC):
@@ -830,13 +837,17 @@
     sums[400:424, 0:128] = total
     sums[400:424, 128:256] = jnp.zeros_like(total)
 
+    wait_sent(1)
+    wait_x_sent(2)
     wait_x(3)
     wait_r(1)
-    wait_e_sent(1)
     left = depth_rows(3, 1, XC)
     for x in range(XC):
         total = depth_synthesise(3, 1, x, left) + base[x]
         fields[1, :, x] = total.reshape(C, YC, 512).astype(BF16)
+    wait_x_sent(3)
+    wait_e_sent(0)
+    wait_e_sent(1)
 
 
 GROUPS = 5
@@ -905,9 +916,11 @@
     fields, sums = pl.pallas_call(
         kernel,
         out_shape=(jax.ShapeDtypeStruct((2,) + block.shape, BF16), jax.ShapeDtypeStruct((424, 256), F32)),
-        in_specs=[vmem] * 4 + [hbm] * 12,
+        in_specs=[hbm] * 2 + [vmem] * 2 + [hbm] * 12,
         out_specs=(vmem,) * 2,
         scratch_shapes=[
+            pltpu.VMEM(block.shape, BF16),
+            pltpu.VMEM(block.shape, BF16),
             pltpu.VMEM((2, 144, 512), BF16),
             pltpu.VMEM((2, 2, 256, 512), BF16),
             pltpu.VMEM((2, 2, 512, 256), BF16),
@@ -939,7 +952,7 @@
             pltpu.VMEM((2, 2, GY, 8, 128), F32),
             pltpu.VMEM((3, 24, 128), F32),
             pltpu.VMEM((3, 8, 24, 128), F32),
-            dma((12,)),
+            dma((14,)),
             dma((4, GX)),
             dma((4, GX)),
             dma((2, EXTRA)),

time: 108 us -> 107 us (level)
  no operation moved by 1% of the time
where the time goes in v5:
time: 107 us
  Pallas kernels  106 us (99%)
    pallas_call x1, Pallas kernels, per_device(): pl.pallas_call(kernel, out_shape=(jax.ShapeDtypeStruct((2,) + block.shape...  101 us
    pallas_call x1, Pallas kernels, per_device(): pl.pallas_call(finish, out_shape=(block, block, jax.ShapeDtypeStruct((2,...  4.73 us

profile of v5, /device:TPU:1, one launch (start us, length us, event | category | flops | bytes accessed | tf_op | source)
XLA Modules:
  0.0 106.6 jit_solution(17471549513598948942)
XLA Ops:
  0.6 101.0 %shard_map.191 = (bf16[2,20,4,8,512]{4,3,2,1,0:T(8,128)(2,1)}, f32[424,256]{1,0:T(8,128)}) custom-call(bf16[20,4,8,512]{3,2,1,0:T(8,128)(2,1)} %bitcast.9, bf16[20,4,8,512]{3,2,1,0:T(8,128)(2,1)} %bitcast.10, f32[20,20]{1,0:T(8,128)} %wpt.1, f32[1,20]{1,0:T(1,128)} %bitcast.11, f32[2,20,20,3,4,24]{5,4,3,2,1,0:T(4,128)} %bitcast.8, ...), custom_call_target="tpu_custom_call" | custom-call | tf_op jit(solution)/shard_map/pallas_call | solution.py:916
  101.7 4.7 %shard_map.192 = (bf16[20,4,8,512]{3,2,1,0:T(8,128)(2,1)}, bf16[20,4,8,512]{3,2,1,0:T(8,128)(2,1)}, f32[2,20,20,3,4,24]{5,4,3,2,1,0:T(4,128)}, f32[20,20]{1,0:T(8,128)}, f32[1,20]{1,0:T(1,128)}) custom-call(bf16[2,20,4,8,512]{4,3,2,1,0:T(8,128)(2,1)} %get-tuple-element.12.fields, f32[424,256]{1,0:T(8,128)} %get-tuple-element.13.sums), custom_call_target="tpu_custom_call" | custom-call | tf_op jit(solution)/shard_map/pallas_call | solution.py:978

commit v6 on v5

--- a/solution.py
+++ b/solution.py
@@ -316,6 +316,7 @@
 
         over(EXTRA, go)
 
+    def wait_r_sent(f):
         @pl.when(special)
         def _():
             over(GX, lambda k: r_copy(f, (d + k) & (GX - 1), which).wait_send(), 1)
@@ -764,9 +765,9 @@
         g = (gpre[0, x], gpre[1, x])
         base[x] = dot3(point_t, g)
         cross += dot(g[0], vb[x], NTD) + dot(g[1], vb[x], NTD)
+    row = lax.broadcasted_iota(jnp.int32, (40, ROWS), 0)
     gather = (
-        lax.broadcasted_iota(jnp.int32, (24, ROWS), 1) // YC
-        == lax.broadcasted_iota(jnp.int32, (24, ROWS), 0)
+        lax.broadcasted_iota(jnp.int32, (40, ROWS), 1) // YC == 5 * lax.rem(row, 8) + row // 8
     ).astype(F32)
     place = (
         lax.broadcasted_iota(jnp.int32, (ROWS, 128), 0) // YC
@@ -774,7 +775,11 @@
     ).astype(F32)
     lane = lax.broadcasted_iota(jnp.int32, (ROWS, 128), 1)
     both = exact(jnp.where(same_y, cross, 0.0), place) + jnp.where(lane == C, row_sum, 0.0)
-    small[0] = exact(gather, both)
+    parts = exact(gather, both)
+    packed = parts[0:8]
+    for m in range(1, 5):
+        packed = packed + pltpu.roll(parts[8 * m : 8 * m + 8], 24 * m, 1)
+    small[0] = packed
 
     def small_copy(s, k, peer, slot):
         return remote(small.at[s], smalls.at[s, slot], ss_sem.at[s, k], rs_sem.at[s, slot], *peer)
@@ -834,8 +839,8 @@
     cells_back(1, 3)
 
     total = finish_small(2)
-    sums[400:424, 0:128] = total
-    sums[400:424, 128:256] = jnp.zeros_like(total)
+    sums[400:408, 0:128] = total
+    sums[400:408, 128:256] = jnp.zeros_like(total)
 
     wait_sent(1)
     wait_x_sent(2)
@@ -846,14 +851,15 @@
         total = depth_synthesise(3, 1, x, left) + base[x]
         fields[1, :, x] = total.reshape(C, YC, 512).astype(BF16)
     wait_x_sent(3)
-    wait_e_sent(0)
-    wait_e_sent(1)
+    for f in range(2):
+        wait_e_sent(f)
+        wait_r_sent(f)
 
 
 GROUPS = 5
 
 
-def finish(fields, sums, act, ghist, gs, gpoint, goff, modes, gs_v, io_sem, gs_sem):
+def finish(fields, sums, act, ghist, gs, gpoint, goff, table, modes, gs_v, io_sem, gs_sem):
     grads = sums.at[80:400]
     copies = [
         pltpu.make_async_copy(fields.at[0], act, io_sem.at[0]),
@@ -861,8 +867,13 @@
     ]
     for copy in copies:
         copy.start()
-    gpoint[...] = sums[400 : 400 + C, 0:C]
-    column = sums[400 : 400 + C, C : C + 1]
+    for m in range(5):
+        packed = sums[400:408, 0:128]
+        packed = packed if m == 0 else pltpu.roll(packed, 128 - 24 * m, 1)
+        for r in range(4):
+            table[5 * r + m : 5 * r + m + 1, :] = packed[r : r + 1]
+    gpoint[...] = table[0:C, 0:C]
+    column = table[0:C, C : C + 1]
     diagonal = lax.broadcasted_iota(jnp.int32, (C, C), 0) == lax.broadcasted_iota(
         jnp.int32, (C, C), 1
     )
@@ -915,7 +926,7 @@
     dma = pltpu.SemaphoreType.DMA
     fields, sums = pl.pallas_call(
         kernel,
-        out_shape=(jax.ShapeDtypeStruct((2,) + block.shape, BF16), jax.ShapeDtypeStruct((424, 256), F32)),
+        out_shape=(jax.ShapeDtypeStruct((2,) + block.shape, BF16), jax.ShapeDtypeStruct((408, 256), F32)),
         in_specs=[hbm] * 2 + [vmem] * 2 + [hbm] * 12,
         out_specs=(vmem,) * 2,
         scratch_shapes=[
@@ -950,8 +961,8 @@
             pltpu.VMEM((2, 2, 2, GY, 8, 128), F32),
             pltpu.VMEM((2, GY, 2, 8, 128), F32),
             pltpu.VMEM((2, 2, GY, 8, 128), F32),
-            pltpu.VMEM((3, 24, 128), F32),
-            pltpu.VMEM((3, 8, 24, 128), F32),
+            pltpu.VMEM((3, 8, 128), F32),
+            pltpu.VMEM((3, 8, 8, 128), F32),
             dma((14,)),
             dma((4, GX)),
             dma((4, GX)),
@@ -983,7 +994,8 @@
         in_specs=[vmem, vmem],
         out_specs=(hbm,) * 3 + (vmem,) * 2,
         scratch_shapes=[
-            pltpu.VMEM((C * 16, 256), F32), pltpu.VMEM((2, C, C, KX, Q, MY), F32), dma((2,)), dma((2, GROUPS)),
+            pltpu.VMEM((24, 128), F32), pltpu.VMEM((C * 16, 256), F32),
+            pltpu.VMEM((2, C, C, KX, Q, MY), F32), dma((2,)), dma((2, GROUPS)),
         ],
         compiler_params=pltpu.CompilerParams(vmem_limit_bytes=60 * 1024 * 1024),
     )(fields, sums)

time: 107 us -> 106 us (level)
  no operation moved by 1% of the time
where the time goes in v6:
time: 106 us
  Pallas kernels  105 us (99%)
    pallas_call x1, Pallas kernels, per_device(): pl.pallas_call(kernel, out_shape=(jax.ShapeDtypeStruct((2,) + block.shape...  100 us
    pallas_call x1, Pallas kernels, per_device(): pl.pallas_call(finish, out_shape=(block, block, jax.ShapeDtypeStruct((2,...  4.73 us

profile of v6, /device:TPU:1, one launch (start us, length us, event | category | flops | bytes accessed | tf_op | source)
XLA Modules:
  0.0 105.6 jit_solution(6306383001663412524)
XLA Ops:
  0.6 100.3 %shard_map.191 = (bf16[2,20,4,8,512]{4,3,2,1,0:T(8,128)(2,1)}, f32[408,256]{1,0:T(8,128)}) custom-call(bf16[20,4,8,512]{3,2,1,0:T(8,128)(2,1)} %bitcast.9, bf16[20,4,8,512]{3,2,1,0:T(8,128)(2,1)} %bitcast.10, f32[20,20]{1,0:T(8,128)} %wpt.1, f32[1,20]{1,0:T(1,128)} %bitcast.11, f32[2,20,20,3,4,24]{5,4,3,2,1,0:T(4,128)} %bitcast.8, ...), custom_call_target="tpu_custom_call" | custom-call | tf_op jit(solution)/shard_map/pallas_call | solution.py:927
  100.9 4.7 %shard_map.192 = (bf16[20,4,8,512]{3,2,1,0:T(8,128)(2,1)}, bf16[20,4,8,512]{3,2,1,0:T(8,128)(2,1)}, f32[2,20,20,3,4,24]{5,4,3,2,1,0:T(4,128)}, f32[20,20]{1,0:T(8,128)}, f32[1,20]{1,0:T(1,128)}) custom-call(bf16[2,20,4,8,512]{4,3,2,1,0:T(8,128)(2,1)} %get-tuple-element.12.fields, f32[408,256]{1,0:T(8,128)} %get-tuple-element.13.sums), custom_call_target="tpu_custom_call" | custom-call | tf_op jit(solution)/shard_map/pallas_call | solution.py:989
